TPU v7x, 32 devices: a whole 2x2x4 slice. The times are simulated.
32 devices in a mesh: section: 2 (over y), dp: 16 (over z, x, core).
Axes of the slice: x: 2, y: 2, z: 4, core: 2. Of those that a mesh axis runs over, the one named last changes fastest.
Arguments:
- layer_input: bfloat16 [2, 4096, 4, 128], P('section', 'dp'), may hold values from 0 to 1
- gate_weight: bfloat16 [2, 4096, 16384], P('section', None, 'dp'), may hold values from -0.09375 to 0.09375
- up_weight: bfloat16 [2, 4096, 16384], P('section', None, 'dp'), may hold values from -0.09375 to 0.09375
- down_weight: bfloat16 [2, 16384, 4096], P('section', 'dp'), may hold values from -0.046875 to 0.046875
- hidden_threshold: int32 [2, 16384], P('section', 'dp'), may hold values from 1 to 5
- hidden_width: int32 [2, 16384], P('section', 'dp'), may hold values from 1 to 5
- out_threshold: int32 [2, 4096], P('section', 'dp'), may hold values from 1 to 5
- out_width: int32 [2, 4096], P('section', 'dp'), may hold values from 1 to 5
- out_cotangent: bfloat16 [2, 4096, 4, 128], P('section', 'dp'), may hold values from -6 to 6
Outputs:
- incoming_spikes: bfloat16 [2, 4096, 4, 128], P('section', 'dp')
- returned_grads: bfloat16 [2, 4096, 4, 128], P('section', 'dp')
All inputs are finite; a program needn't handle non-finite values.
Results may differ from a plain program's by a relative error of at most 0.013.
Values may be sent and summed in bfloat16 or wider, within the bound.
No kernel may reach another device: no remote copies, remote signals or barrier semaphores. Data moves between devices by JAX's collectives and lax.ppermute only.
A program may use at most 128 MiB of HBM per device.

v0:
```python
import functools

import jax
import jax.numpy as jnp
from jax import lax
from jax.experimental import pallas as pl
from jax.experimental.pallas import tpu as pltpu
from jax.sharding import PartitionSpec as P

decay_rate = 0.9
level_unit = 0.125
f32 = jnp.float32
bf16 = jnp.bfloat16
VMEM_LIMIT = 8 * 1024 * 1024


def in_vmem(x):
    return pltpu.with_memory_space_constraint(x, pltpu.VMEM)


def call(kernel, outs, *args, flops=0, aliases=None, fetch=()):
    specs = []
    given = []
    for a in args:
        if a.dtype == jnp.int32 and a.ndim == 1:
            specs.append(pl.BlockSpec(memory_space=pltpu.SMEM))
            given.append(a)
        else:
            specs.append(pl.BlockSpec(memory_space=pltpu.VMEM))
            given.append(in_vmem(a))
    n_in, n_out, n_fetch = len(args), len(outs), len(fetch)
    specs += [pl.BlockSpec(memory_space=pltpu.HBM)] * n_fetch
    given += [pltpu.with_memory_space_constraint(w, pltpu.HBM) for w in fetch]
    outs = list(outs) + [(w.shape, w.dtype) for w in fetch]

    def body(*refs):
        ins, sources, refs = refs[:n_in], refs[n_in : n_in + n_fetch], refs[n_in + n_fetch :]
        copies = [
            pltpu.make_async_copy(sources[w], refs[n_out + w], refs[n_out + n_fetch].at[w])
            for w in range(n_fetch)
        ]
        for copy in copies:
            copy.start()
        if kernel is not None:
            kernel(*ins, *refs[:n_out])
        for copy in copies:
            copy.wait()

    res = pl.pallas_call(
        body,
        out_shape=[pltpu.VMEM(shape, dtype) for shape, dtype in outs],
        in_specs=specs,
        out_specs=[pl.BlockSpec(memory_space=pltpu.VMEM)] * len(outs),
        scratch_shapes=[pltpu.SemaphoreType.DMA((n_fetch,))] if n_fetch else [],
        input_output_aliases=aliases or {},
        compiler_params=pltpu.CompilerParams(vmem_limit_bytes=VMEM_LIMIT),
        cost_estimate=pl.CostEstimate(flops=max(flops, 1), bytes_accessed=max(flops // 512, 1), transcendentals=0),
    )(*given)
    return list(res[:n_out]), list(res[n_out:])


def nn(left, right):
    return lax.dot_general(left, right, (((1,), (0,)), ((), ())), preferred_element_type=f32)


def nt(left, right):
    return lax.dot_general(left, right, (((1,), (1,)), ((), ())), preferred_element_type=f32)


def over_tiles(total, width, work):
    width = min(width, total)

    def body(k, carry):
        work(pl.ds(pl.multiple_of(k * width, width), width))
        return carry

    lax.fori_loop(0, total // width, body, 0)


def levels(threshold_ref, width_ref, at):
    threshold = level_unit * threshold_ref[:, at].astype(f32)
    scale = 1.0 / (level_unit * width_ref[:, at].astype(f32))
    return threshold, scale


def sigmoid(v):
    return 0.5 * jnp.tanh(0.5 * v) + 0.5


def spikes_of(currents, threshold, scale):
    potential = None
    out = []
    for current in currents:
        if potential is None:
            potential = current
        else:
            potential = decay_rate * (potential - threshold * out[-1]) + current
        out.append(sigmoid((potential - threshold) * scale))
    return out


def slopes_of(spikes, scale):
    return [v * (1.0 - v) * scale for v in spikes]


def spikes_back(slopes, cotangents, threshold):
    after = None
    grads = [None] * len(slopes)
    for t in reversed(range(len(slopes))):
        if after is None:
            after = cotangents[t] * slopes[t]
        else:
            after = (cotangents[t] - decay_rate * threshold * after) * slopes[t] + decay_rate * after
        grads[t] = after
    return grads


def tied(value, after):
    return lax.optimization_barrier((value, after))[0]


def step_rows(count, tokens):
    return [slice(t * tokens, (t + 1) * tokens) for t in range(count)]


def whole_pieces(refs, shape):
    out = []
    pending = None
    for ref in refs:
        if ref.shape == shape:
            out.append(ref[...])
        elif pending is None:
            pending = ref[...]
        else:
            out.append(jnp.concatenate([pending, ref[...]], axis=0))
            pending = None
    return out


def block_of(spot, local, chips):
    index = lax.axis_index("dp")
    chip, core = index // 2, index % 2
    side = chips // 2
    place = jnp.where(chip % 2 == 0, chip // 2, chips - 1 - chip // 2)
    place = (place + spot // 2) % chips
    chip = jnp.where(place < side, 2 * place, 2 * (chips - 1 - place) + 1)
    core = 1 - core if spot % 2 else core
    return pl.ds(pl.multiple_of((2 * chip + core) * local, local), local)


def turn_kernel(raw, out):
    tokens = raw.shape[2]
    for t in range(raw.shape[1]):
        out[t * tokens : (t + 1) * tokens, :] = raw[:, t, :].astype(f32).T.astype(out.dtype)


def turned(raw):
    shape = (raw.shape[1] * raw.shape[2], raw.shape[0])
    return call(turn_kernel, [(shape, raw.dtype)], raw)[0][0]


def gate_up_kernel(chips, spots, n_pieces, first, last, steps, tokens, *refs):
    refs = list(refs)
    piece_refs, refs = refs[:n_pieces], refs[n_pieces:]
    weights, refs = refs[:2], refs[2:]
    if not first:
        acc, refs = refs[:2], refs[2:]
    if last:
        threshold_ref, width_ref = refs[:2]
        refs = refs[2:]
    local = piece_refs[0].shape[1]
    blocks = [block_of(p, local, chips) for p in spots]

    def work(cols):
        left = jnp.concatenate(whole_pieces(piece_refs, (steps * tokens, local)), axis=1)
        both = []
        for which in range(2):
            right = jnp.concatenate([weights[which][here, cols] for here in blocks], axis=0)
            total = nn(left, right)
            if not first:
                total = total + acc[which][:, cols]
            both.append(total)
            refs[which][:, cols] = total
        if last:
            threshold, scale = levels(threshold_ref, width_ref, cols)
            hidden = both[0] * sigmoid(both[0]) * both[1]
            parts = [hidden[r] for r in step_rows(steps, tokens)]
            out = spikes_of(parts, threshold, scale)
            refs[2][:, cols] = jnp.concatenate(out, axis=0).astype(bf16)

    over_tiles(refs[0].shape[1], 512, work)


def down_kernel(chips, spots, spikes, down, *outs):
    left = spikes[...]
    for p, out in zip(spots, outs):
        out[...] = nn(left, down[:, block_of(p, out.shape[1], chips)]).astype(out.dtype)


def out_kernel(steps, tokens, own, sib, fw, bw, x, cot, threshold_ref, width_ref, emitted, grad, grad16):
    threshold, scale = levels(threshold_ref, width_ref, slice(None))
    current = (
        own[...] + sib[...].astype(f32) + fw[...].astype(f32) + bw[...].astype(f32) + x[...].astype(f32)
    )
    rows = step_rows(steps, tokens)
    out = spikes_of([current[r] for r in rows], threshold, scale)
    emitted[...] = jnp.concatenate(out, axis=0).astype(bf16)
    grads = spikes_back(slopes_of(out, scale), [cot[r, :].astype(f32) for r in rows], threshold)
    total = jnp.concatenate(grads, axis=0)
    grad[...] = total
    grad16[...] = total.astype(bf16)


def spike_grad_kernel(chips, spots, n_pieces, first, last, steps, tokens, *refs):
    refs = list(refs)
    piece_refs, refs = refs[:n_pieces], refs[n_pieces:]
    down, refs = refs[0], refs[1:]
    if not first:
        acc, refs = refs[0], refs[1:]
    if last:
        slope, to_gate, to_up, threshold_ref, width_ref = refs[:5]
        refs = refs[5:]
    local = piece_refs[0].shape[1]
    blocks = [block_of(p, local, chips) for p in spots]

    def work(hid):
        left = jnp.concatenate(whole_pieces(piece_refs, (steps * tokens, local)), axis=1)
        total = nt(left, jnp.concatenate([down[hid, here] for here in blocks], axis=1))
        if not first:
            total = total + acc[:, hid]
        if not last:
            refs[0][:, hid] = total
            return
        threshold, _ = levels(threshold_ref, width_ref, hid)
        parts = step_rows(steps, tokens)
        grads = spikes_back([slope[r, hid] for r in parts], [total[r] for r in parts], threshold)
        grad = jnp.concatenate(grads, axis=0)
        refs[0][:, hid] = (grad * to_gate[:, hid]).astype(bf16)
        refs[1][:, hid] = (grad * to_up[:, hid]).astype(bf16)

    over_tiles(down.shape[0], 512, work)


def slopes_kernel(steps, tokens, gate, up, threshold_ref, width_ref, slope, to_gate, to_up):
    def work(hid):
        threshold, scale = levels(threshold_ref, width_ref, hid)
        gate_in, up_in = gate[:, hid], up[:, hid]
        sig = sigmoid(gate_in)
        act = gate_in * sig
        hidden = act * up_in
        parts = step_rows(steps, tokens)
        out = spikes_of([hidden[r] for r in parts], threshold, scale)
        slope[:, hid] = jnp.concatenate(slopes_of(out, scale), axis=0)
        to_gate[:, hid] = up_in * (sig * (1.0 + gate_in * (1.0 - sig)))
        to_up[:, hid] = act

    over_tiles(gate.shape[1], 256, work)


def input_grad_kernel(chips, spots, gate_grad, up_grad, gate_w, up_w, *outs):
    left = jnp.concatenate([gate_grad[...], up_grad[...]], axis=1)
    for p, out in zip(spots, outs):
        here = block_of(p, out.shape[1], chips)
        right = jnp.concatenate([gate_w[here, :], up_w[here, :]], axis=1)
        out[...] = nt(left, right).astype(out.dtype)


def per_device(
    devices,
    layer_input,
    gate_weight,
    up_weight,
    down_weight,
    hidden_threshold,
    hidden_width,
    out_threshold,
    out_width,
    out_cotangent,
):
    local = layer_input.shape[1]
    steps = layer_input.shape[2]
    tokens = layer_input.shape[3]
    rows = steps * tokens
    half = rows // 2
    hid = gate_weight.shape[2]
    chips = devices // 2
    far = chips // 2
    side = chips // 2

    order = [2 * p if p < side else 2 * (chips - 1 - p) + 1 for p in range(chips)]
    forward, backward, sibling = [], [], []
    for p in range(chips):
        a, b = order[p], order[(p + 1) % chips]
        for core in range(2):
            forward.append((2 * a + core, 2 * b + core))
            backward.append((2 * b + core, 2 * a + core))
            sibling.append((2 * a + core, 2 * a + 1 - core))
    send_fw = lambda v: lax.ppermute(v, "dp", forward)
    send_bw = lambda v: lax.ppermute(v, "dp", backward)
    swap = lambda v: lax.ppermute(v, "dp", sibling)

    x = turned(layer_input[0])
    cot = turned(out_cotangent[0])

    gate_hbm, up_hbm, down_hbm = gate_weight[0], up_weight[0], down_weight[0]
    spots = lambda at: [(d % chips) * 2 + s for d, s in at]

    def gathered(mine, take, beside):
        held, own, sib = None, [], []
        fw = bw = mine

        def taken(new, last=False):
            pieces = [p for v, _ in new for p in (v if isinstance(v, tuple) else (v,))]
            return take(pieces, [at for _, at in new], held, last)

        def swapped(new):
            return [
                (tuple(map(swap, v)) if isinstance(v, tuple) else swap(v), (d, True)) for v, (d, _) in new
            ]

        for k in range(1, far + 1):
            sent = (fw[:half], bw[half:]) if k == far else (fw, bw)
            next_fw, next_bw = send_fw(sent[0]), send_bw(sent[1])
            if k == 1:
                own = [(mine, (0, False))]
                sib = own + swapped(own)
            else:
                own = [(fw, (1 - k, False)), (bw, (k - 1, False))]
                held, sib = taken(own + sib), swapped(own)
            fw, bw = next_fw, next_bw
            fw, held, _ = lax.optimization_barrier((fw, held, beside.get(k)))
            bw = tied(bw, held)
        own = [((fw, bw), (-far, False))]
        last = swapped(own)
        held = taken(own + sib)
        return taken(last, last=True)

    def scattered(blocks_of, parts):
        def group(k):
            return [(d, s) for s in (False, True) for d in ([k, -k] if k else [0])]

        def sums(own, sib):
            return [o + s.astype(f32) for o, s in zip(own, sib)]

        sib = swap(blocks_of([(far, True)], None)[0])
        first = blocks_of([(far, False)] + group(far - 1)[2:], None)
        total = first[0] + sib.astype(f32)
        fw, bw = total[:half].astype(bf16), total[half:].astype(bf16)
        now_own, now_sib = None, first[1:]
        cut = [slice(p * rows // parts, (p + 1) * rows // parts) for p in range(parts)]
        for k in range(1, far):
            after = fw, bw
            fw, bw = send_fw(fw), send_bw(bw)
            now_sib = [swap(v) for v in now_sib]
            if k == 1:
                now_own = blocks_of(group(far - 1)[:2], after)
                fw, now_own = lax.optimization_barrier((fw, now_own))
            later = blocks_of(group(far - k - 1), after)
            fw, later = lax.optimization_barrier((fw, later))
            bw = tied(bw, later)
            a, b = sums(now_own, now_sib)
            if k == 1:
                fw = jnp.concatenate([a[:half] + fw.astype(f32), a[half:]], axis=0).astype(bf16)
                bw = jnp.concatenate([b[:half], b[half:] + bw.astype(f32)], axis=0).astype(bf16)
            else:
                fw, bw = (a + fw.astype(f32)).astype(bf16), (b + bw.astype(f32)).astype(bf16)
            now_own, now_sib = later[: len(later) // 2], later[len(later) // 2 :]
        ends = [(send_fw(fw[c]), send_bw(bw[c])) for c in cut]
        return now_own[0], swap(now_sib[0]), [e[0] for e in ends], [e[1] for e in ends], cut

    hid_level, hid_spread = hidden_threshold, hidden_width
    gate_w, up_w = call(None, [], fetch=(tied(gate_hbm, x), up_hbm))[1]
    down_w = None

    def take_inputs(pieces, at, acc, last):
        nonlocal down_w
        first = acc is None
        args = [*pieces, gate_w, up_w]
        aliases = {}
        if not first:
            aliases = {len(args): 0, len(args) + 1: 1}
            args += list(acc)
        outs = [((rows, hid), f32)] * 2
        if last:
            args += [hid_level, hid_spread]
            outs = outs + [((rows, hid), bf16)]
        res, new = call(
            functools.partial(gate_up_kernel, chips, spots(at), len(pieces), first, last, steps, tokens),
            outs,
            *args,
            flops=0,
            aliases=aliases,
            fetch=(down_hbm,) if first else (),
        )
        if new:
            down_w = new[0]
        return res

    gate, upward, spikes = gathered(x, take_inputs, {1: (gate_w, up_w)})

    def blocks(kernel, flops, *args):
        def blocks_of(at, after):
            outs = [((rows, local), bf16 if s else f32) for _, s in at]
            first = args[0] if after is None else tied(args[0], after)
            return call(functools.partial(kernel, chips, spots(at)), outs, first, *args[1:], flops=len(at) * flops)[0]

        return blocks_of

    own, sib, fw, bw, _ = scattered(blocks(down_kernel, 2 * rows * hid * local, spikes, down_w), 1)
    (emitted, current_grad, grad16), _ = call(
        functools.partial(out_kernel, steps, tokens),
        [((rows, local), bf16), ((rows, local), f32), ((rows, local), bf16)],
        own, sib, fw[0], bw[0], x, cot, out_threshold, out_width,
    )

    sections = lax.axis_size("section")
    incoming = lax.ppermute(emitted, "section", [(s, s + 1) for s in range(sections - 1)])
    way_back, _ = call(
        functools.partial(slopes_kernel, steps, tokens),
        [((rows, hid), f32)] * 3,
        tied(gate, grad16), upward, hid_level, hid_spread,
        flops=2 * rows * hid * local,
    )

    def take_grads(pieces, at, acc, last):
        first = acc is None
        args = [*pieces, down_w]
        aliases = {}
        if not first:
            if not last:
                aliases = {len(args): 0}
            args += acc
        outs = [((rows, hid), f32)]
        if last:
            args += [*way_back, hid_level, hid_spread]
            outs = [((rows, hid), bf16)] * 2
        return call(
            functools.partial(spike_grad_kernel, chips, spots(at), len(pieces), first, last, steps, tokens),
            outs,
            *args,
            flops=2 * rows * hid * local * len(at),
            aliases=aliases,
        )[0]

    gate_grad, up_grad = gathered(grad16, take_grads, {1: way_back})

    own, sib, fw, bw, cut = scattered(
        blocks(input_grad_kernel, 4 * rows * hid * local, gate_grad, up_grad, gate_w, up_w), 1
    )
    returned = []
    for c, from_fw, from_bw in zip(cut, fw, bw):
        total = own[c] + sib[c].astype(f32) + current_grad[c] + from_fw.astype(f32) + from_bw.astype(f32)
        returned.append(
            lax.ppermute(total.astype(bf16), "section", [(s + 1, s) for s in range(sections - 1)])
        )

    def viewed(v):
        return jnp.transpose(v.reshape(steps, tokens, local), (2, 0, 1))[None]

    return viewed(incoming), viewed(jnp.concatenate(returned, axis=0))


def solution(mesh):
    placed = (
        P("section", "dp", None, None),
        P("section", None, "dp"),
        P("section", None, "dp"),
        P("section", "dp", None),
        P("section", "dp"),
        P("section", "dp"),
        P("section", "dp"),
        P("section", "dp"),
        P("section", "dp", None, None),
    )
    return jax.shard_map(
        functools.partial(per_device, mesh.shape["dp"]),
        mesh=mesh,
        in_specs=placed,
        out_specs=(P("section", "dp", None, None), P("section", "dp", None, None)),
        check_vma=False,
    )
```

profile of v0, /device:TPU:0, one launch (start us, length us, event | category | flops | bytes accessed | tf_op | source)
XLA Modules:
  0.0 150.1 jit_solution(16382725992706546331)
XLA Ops:
  2.1 3.1 %collective-permute-start = (bf16[512,256]{1,0:T(8,128)(2,1)S(1)}, bf16[512,256]{1,0:T(8,128)(2,1)S(1)}, u32[]{:S(2)}, u32[]{:S(2)}) collective-permute-start(bf16[512,256]{1,0:T(8,128)(2,1)S(1)} %shard_map.104.refs_2_.refs_4_), channel_id=1, source_target_pairs={{0,4},{1,5},{4,8},{5,9},{8,12},{9,13},{12,14},{13,15},{14,10},{15,... | collective-permute-start | bytes 786440 | tf_op jit(solution)/shard_map/ppermute | solution.py:298
  5.1 5.8 %shard_map.105 = (bf16[4096,1024]{1,0:T(8,128)(2,1)S(1)}, bf16[4096,1024]{1,0:T(8,128)(2,1)S(1)}) custom-call(bf16[4096,1024]{1,0:T(8,128)(2,1)} %bitcast.16, bf16[4096,1024]{1,0:T(8,128)(2,1)} %bitcast.17), custom_call_target="tpu_custom_call" | custom-call | flops 1 | bytes 1 | tf_op jit(solution)/shard_map/pallas_call | solution.py:49
  13.9 3.4 %shard_map.106 = (f32[512,1024]{1,0:T(8,128)S(1)}, f32[512,1024]{1,0:T(8,128)S(1)}, bf16[1024,4096]{1,0:T(8,128)(2,1)S(1)}) custom-call(bf16[512,256]{1,0:T(8,128)(2,1)S(1)} %collective-permute-done.refs_0_, bf16[512,256]{1,0:T(8,128)(2,1)S(1)} %collective-permute-done.2.refs_1_, bf16[512,256]{1,0:T(8,128)(2,1)S(1)} %shard_map.104.refs_2_.refs_4_, ...), custom_call_target="tpu_custom_call" | custom-call | flops 1 | bytes 1 | tf_op jit(solution)/shard_map/pallas_call | solution.py:49
  17.3 2.6 %collective-permute-done.1.refs_0_ = bf16[512,256]{1,0:T(8,128)(2,1)S(1)} collective-permute-done((bf16[512,256]{1,0:T(8,128)(2,1)S(1)}, bf16[512,256]{1,0:T(8,128)(2,1)S(1)}, u32[]{:S(2)}, u32[]{:S(2)}) %collective-permute-start.1) | collective-permute-done | bytes 262176 | tf_op jit(solution)/shard_map/ppermute | solution.py:298
  22.5 2.8 %shard_map.107 = (f32[512,1024]{1,0:T(8,128)S(1)}, f32[512,1024]{1,0:T(8,128)S(1)}) custom-call(bf16[512,256]{1,0:T(8,128)(2,1)S(1)} %collective-permute-done.1.refs_0_, bf16[512,256]{1,0:T(8,128)(2,1)S(1)} %collective-permute-done.5.refs_1_, bf16[512,256]{1,0:T(8,128)(2,1)S(1)} %collective-permute-done.6.refs_2_, ...), custom_call_target="tpu_custom_call", output_to_operand_aliasing={{0}: (6, {}), {1}: (7, {})} | custom-call | flops 1 | bytes 1 | tf_op jit(solution)/shard_map/pallas_call | solution.py:49
  25.2 2.5 %collective-permute-done.4.refs_0_ = bf16[512,256]{1,0:T(8,128)(2,1)S(1)} collective-permute-done((bf16[512,256]{1,0:T(8,128)(2,1)S(1)}, bf16[512,256]{1,0:T(8,128)(2,1)S(1)}, u32[]{:S(2)}, u32[]{:S(2)}) %collective-permute-start.4) | collective-permute-done | bytes 262176 | tf_op jit(solution)/shard_map/ppermute | solution.py:298
  27.7 1.9 %collective-permute-start.8 = (bf16[256,256]{1,0:T(8,128)(2,1)S(1)}, bf16[256,256]{1,0:T(8,128)(2,1)S(1)}, u32[]{:S(2)}, u32[]{:S(2)}) collective-permute-start(bf16[256,256]{1,0:T(8,128)(2,1)S(1)} %slice.56), channel_id=1, source_target_pairs={{0,4},{1,5},{4,8},{5,9},{8,12},{9,13},{12,14},{13,15},{14,10},{15,... | collective-permute-start | bytes 393224 | tf_op jit(solution)/shard_map/ppermute | solution.py:298
  30.3 2.7 %shard_map.108 = (f32[512,1024]{1,0:T(8,128)S(1)}, f32[512,1024]{1,0:T(8,128)S(1)}) custom-call(bf16[512,256]{1,0:T(8,128)(2,1)S(1)} %collective-permute-done.4.refs_0_, bf16[512,256]{1,0:T(8,128)(2,1)S(1)} %collective-permute-done.9.refs_1_, bf16[512,256]{1,0:T(8,128)(2,1)S(1)} %collective-permute-done.10.refs_2_, ...), custom_call_target="tpu_custom_call", output_to_operand_aliasing={{0}: (6, {}), {1}: (7, {})} | custom-call | flops 1 | bytes 1 | tf_op jit(solution)/shard_map/pallas_call | solution.py:49
  35.1 2.2 %shard_map.109 = (f32[512,1024]{1,0:T(8,128)S(1)}, f32[512,1024]{1,0:T(8,128)S(1)}) custom-call(bf16[256,256]{1,0:T(8,128)(2,1)S(1)} %collective-permute-done.8.refs_0_, bf16[256,256]{1,0:T(8,128)(2,1)S(1)} %collective-permute-done.13.refs_1_, bf16[512,256]{1,0:T(8,128)(2,1)S(1)} %collective-permute-done.15.refs_2_, ...), custom_call_target="tpu_custom_call", output_to_operand_aliasing={{0}: (6, {}), {1}: (7, {})} | custom-call | flops 1 | bytes 1 | tf_op jit(solution)/shard_map/pallas_call | solution.py:49
  37.4 1.9 %shard_map.110 = (f32[512,1024]{1,0:T(8,128)S(1)}, f32[512,1024]{1,0:T(8,128)S(1)}, bf16[512,1024]{1,0:T(8,128)(2,1)S(1)}) custom-call(bf16[256,256]{1,0:T(8,128)(2,1)S(1)} %collective-permute-done.12.refs_0_, bf16[256,256]{1,0:T(8,128)(2,1)S(1)} %collective-permute-done.14.refs_1_, ...), custom_call_target="tpu_custom_call", output_to_operand_aliasing={{0}: (4, {}), {1}: (5, {})} | custom-call | flops 1 | bytes 1 | tf_op jit(solution)/shard_map/pallas_call | solution.py:49
  53.0 3.7 %collective-permute-done.21 = bf16[512,256]{1,0:T(8,128)(2,1)S(1)} collective-permute-done((bf16[512,256]{1,0:T(8,128)(2,1)S(1)}, bf16[512,256]{1,0:T(8,128)(2,1)S(1)}, u32[]{:S(2)}, u32[]{:S(2)}) %collective-permute-start.21) | collective-permute-done | bytes 262176 | tf_op jit(solution)/shard_map/ppermute | solution.py:298
  61.7 2.8 %collective-permute-done.24 = bf16[512,256]{1,0:T(8,128)(2,1)S(1)} collective-permute-done((bf16[512,256]{1,0:T(8,128)(2,1)S(1)}, bf16[512,256]{1,0:T(8,128)(2,1)S(1)}, u32[]{:S(2)}, u32[]{:S(2)}) %collective-permute-start.24) | collective-permute-done | bytes 262176 | tf_op jit(solution)/shard_map/ppermute | solution.py:298
  64.5 2.0 %collective-permute-done.31 = bf16[512,256]{1,0:T(8,128)(2,1)S(1)} collective-permute-done((bf16[512,256]{1,0:T(8,128)(2,1)S(1)}, bf16[512,256]{1,0:T(8,128)(2,1)S(1)}, u32[]{:S(2)}, u32[]{:S(2)}) %collective-permute-start.31) | collective-permute-done | bytes 262176 | tf_op jit(solution)/shard_map/ppermute | solution.py:299
  69.3 3.7 %collective-permute-done.32.refs_3_ = bf16[512,256]{1,0:T(8,128)(2,1)S(1)} collective-permute-done((bf16[512,256]{1,0:T(8,128)(2,1)S(1)}, bf16[512,256]{1,0:T(8,128)(2,1)S(1)}, u32[]{:S(2)}, u32[]{:S(2)}) %collective-permute-start.32) | collective-permute-done | bytes 262176 | tf_op jit(solution)/shard_map/ppermute | solution.py:299
  74.3 2.5 %collective-permute-start.34 = (bf16[512,256]{1,0:T(8,128)(2,1)S(1)}, bf16[512,256]{1,0:T(8,128)(2,1)S(1)}, u32[]{:S(2)}, u32[]{:S(2)}) collective-permute-start(bf16[512,256]{1,0:T(8,128)(2,1)S(1)} %get-tuple-element.187.refs_2_), channel_id=1, source_target_pairs={{0,4},{1,5},{4,8},{5,9},{8,12},{9,13},{12,14},{13,15},{14,10},{15,... | collective-permute-start | bytes 786440 | tf_op jit(solution)/shard_map/ppermute | solution.py:298
  76.8 1.8 %shard_map.119 = (f32[512,1024]{1,0:T(8,128)S(1)}, f32[512,1024]{1,0:T(8,128)S(1)}, f32[512,1024]{1,0:T(8,128)S(1)}) custom-call(f32[512,1024]{1,0:T(8,128)S(1)} %get-tuple-element.189.refs_0_, f32[512,1024]{1,0:T(8,128)S(1)} %get-tuple-element.190.refs_1_, s32[1,1024]{1,0:T(1,128)S(1)} %copy-done.2, s32[1,1024]{1,0:T(1,128)S(1)} %copy-done.3), custom_call_target="tpu_custom_call" | custom-call | flops 268435456 | bytes 524288 | tf_op jit(solution)/shard_map/pallas_call | solution.py:49
  78.7 2.0 %collective-permute-done.34.refs_0_ = bf16[512,256]{1,0:T(8,128)(2,1)S(1)} collective-permute-done((bf16[512,256]{1,0:T(8,128)(2,1)S(1)}, bf16[512,256]{1,0:T(8,128)(2,1)S(1)}, u32[]{:S(2)}, u32[]{:S(2)}) %collective-permute-start.34) | collective-permute-done | bytes 262176 | tf_op jit(solution)/shard_map/ppermute | solution.py:298
  80.7 2.5 %collective-permute-start.35 = (bf16[512,256]{1,0:T(8,128)(2,1)S(1)}, bf16[512,256]{1,0:T(8,128)(2,1)S(1)}, u32[]{:S(2)}, u32[]{:S(2)}) collective-permute-start(bf16[512,256]{1,0:T(8,128)(2,1)S(1)} %collective-permute-done.34.refs_0_), channel_id=1, source_target_pairs={{0,4},{1,5},{4,8},{5,9},{8,12},{9,13},{12,14},{13,15},{14,10},{15,... | collective-permute-start | bytes 786440 | tf_op jit(solution)/shard_map/ppermute | solution.py:298
  85.2 2.2 %collective-permute-done.35.refs_0_ = bf16[512,256]{1,0:T(8,128)(2,1)S(1)} collective-permute-done((bf16[512,256]{1,0:T(8,128)(2,1)S(1)}, bf16[512,256]{1,0:T(8,128)(2,1)S(1)}, u32[]{:S(2)}, u32[]{:S(2)}) %collective-permute-start.35) | collective-permute-done | bytes 262176 | tf_op jit(solution)/shard_map/ppermute | solution.py:298
  87.4 2.1 %collective-permute-start.38 = (bf16[512,256]{1,0:T(8,128)(2,1)S(1)}, bf16[512,256]{1,0:T(8,128)(2,1)S(1)}, u32[]{:S(2)}, u32[]{:S(2)}) collective-permute-start(bf16[512,256]{1,0:T(8,128)(2,1)S(1)} %collective-permute-done.35.refs_0_), channel_id=1, source_target_pairs={{0,4},{1,5},{4,8},{5,9},{8,12},{9,13},{12,14},{13,15},{14,10},{15,... | collective-permute-start | bytes 786440 | tf_op jit(solution)/shard_map/ppermute | solution.py:298
  91.7 2.1 %collective-permute-done.38.refs_0_ = bf16[512,256]{1,0:T(8,128)(2,1)S(1)} collective-permute-done((bf16[512,256]{1,0:T(8,128)(2,1)S(1)}, bf16[512,256]{1,0:T(8,128)(2,1)S(1)}, u32[]{:S(2)}, u32[]{:S(2)}) %collective-permute-start.38) | collective-permute-done | bytes 262176 | tf_op jit(solution)/shard_map/ppermute | solution.py:298
  93.8 2.1 %collective-permute-done.43.refs_1_ = bf16[512,256]{1,0:T(8,128)(2,1)S(1)} collective-permute-done((bf16[512,256]{1,0:T(8,128)(2,1)S(1)}, bf16[512,256]{1,0:T(8,128)(2,1)S(1)}, u32[]{:S(2)}, u32[]{:S(2)}) %collective-permute-start.43) | collective-permute-done | bytes 262176 | tf_op jit(solution)/shard_map/ppermute | solution.py:299
  96.7 1.9 %collective-permute-start.47 = (bf16[256,256]{1,0:T(8,128)(2,1)S(1)}, bf16[256,256]{1,0:T(8,128)(2,1)S(1)}, u32[]{:S(2)}, u32[]{:S(2)}) collective-permute-start(bf16[256,256]{1,0:T(8,128)(2,1)S(1)} %slice.65), channel_id=1, source_target_pairs={{4,0},{5,1},{8,4},{9,5},{12,8},{13,9},{14,12},{15,13},{10,14},{11,... | collective-permute-start | bytes 393224 | tf_op jit(solution)/shard_map/ppermute | solution.py:299
  106.2 1.8 %shard_map.125 = (f32[512,256]{1,0:T(8,128)S(1)}, bf16[512,256]{1,0:T(8,128)(2,1)S(1)}, bf16[512,256]{1,0:T(8,128)(2,1)S(1)}) custom-call(bf16[512,1024]{1,0:T(8,128)(2,1)S(1)} %get-tuple-element.236.refs_0_, bf16[512,1024]{1,0:T(8,128)(2,1)S(1)} %get-tuple-element.205.refs_1_, bf16[4096,1024]{1,0:T(8,128)(2,1)S(1)} %get-tuple-element.124.refs_4_.refs_2_, ...), custom_call_target="tpu_custom_call" | custom-call | flops 1610612736 | bytes 3145728 | tf_op jit(solution)/shard_map/pallas_call | solution.py:49
  110.8 2.4 %shard_map.128 = (f32[512,256]{1,0:T(8,128)S(1)}, f32[512,256]{1,0:T(8,128)S(1)}, bf16[512,256]{1,0:T(8,128)(2,1)S(1)}, bf16[512,256]{1,0:T(8,128)(2,1)S(1)}) custom-call(bf16[512,1024]{1,0:T(8,128)(2,1)S(1)} %get-tuple-element.236.refs_0_, bf16[512,1024]{1,0:T(8,128)(2,1)S(1)} %get-tuple-element.205.refs_1_, ...), custom_call_target="tpu_custom_call" | custom-call | flops 2147483648 | bytes 4194304 | tf_op jit(solution)/shard_map/pallas_call | solution.py:49
  117.8 2.4 %shard_map.129 = (f32[512,256]{1,0:T(8,128)S(1)}, f32[512,256]{1,0:T(8,128)S(1)}, bf16[512,256]{1,0:T(8,128)(2,1)S(1)}, bf16[512,256]{1,0:T(8,128)(2,1)S(1)}) custom-call(bf16[512,1024]{1,0:T(8,128)(2,1)S(1)} %get-tuple-element.236.refs_0_, bf16[512,1024]{1,0:T(8,128)(2,1)S(1)} %get-tuple-element.205.refs_1_, ...), custom_call_target="tpu_custom_call" | custom-call | flops 2147483648 | bytes 4194304 | tf_op jit(solution)/shard_map/pallas_call | solution.py:49
  120.2 3.1 %collective-permute-done.55 = bf16[512,256]{1,0:T(8,128)(2,1)S(1)} collective-permute-done((bf16[512,256]{1,0:T(8,128)(2,1)S(1)}, bf16[512,256]{1,0:T(8,128)(2,1)S(1)}, u32[]{:S(2)}, u32[]{:S(2)}) %collective-permute-start.55) | collective-permute-done | bytes 262176 | tf_op jit(solution)/shard_map/ppermute | solution.py:298
  127.0 5.2 %collective-permute-done.58 = bf16[512,256]{1,0:T(8,128)(2,1)S(1)} collective-permute-done((bf16[512,256]{1,0:T(8,128)(2,1)S(1)}, bf16[512,256]{1,0:T(8,128)(2,1)S(1)}, u32[]{:S(2)}, u32[]{:S(2)}) %collective-permute-start.58) | collective-permute-done | bytes 262176 | tf_op jit(solution)/shard_map/ppermute | solution.py:298
  134.5 3.4 %collective-permute-start.33 = (bf16[512,256]{1,0:T(8,128)(2,1)S(1)}, bf16[512,256]{1,0:T(8,128)(2,1)S(1)}, u32[]{:S(2)}, u32[]{:S(2)}) collective-permute-start(bf16[512,256]{1,0:T(8,128)(2,1)S(1)} %get-tuple-element.186), channel_id=1, source_target_pairs={{0,16},{1,17},{2,18},{3,19},{4,20},{5,21},{6,22},{7,23},{8,24},{9,... | collective-permute-start | bytes 786440 | tf_op jit(solution)/shard_map/ppermute | solution.py:417
  137.9 2.2 %collective-permute-done.63 = bf16[512,256]{1,0:T(8,128)(2,1)S(1)} collective-permute-done((bf16[512,256]{1,0:T(8,128)(2,1)S(1)}, bf16[512,256]{1,0:T(8,128)(2,1)S(1)}, u32[]{:S(2)}, u32[]{:S(2)}) %collective-permute-start.63) | collective-permute-done | bytes 262176 | tf_op jit(solution)/shard_map/ppermute | solution.py:298
  141.8 2.3 %collective-permute-done.33 = bf16[512,256]{1,0:T(8,128)(2,1)S(1)} collective-permute-done((bf16[512,256]{1,0:T(8,128)(2,1)S(1)}, bf16[512,256]{1,0:T(8,128)(2,1)S(1)}, u32[]{:S(2)}, u32[]{:S(2)}) %collective-permute-start.33) | collective-permute-done | bytes 262176 | tf_op jit(solution)/shard_map/ppermute | solution.py:417
  145.0 4.2 %collective-permute-done.67 = bf16[512,256]{1,0:T(8,128)(2,1)S(1)} collective-permute-done((bf16[512,256]{1,0:T(8,128)(2,1)S(1)}, bf16[512,256]{1,0:T(8,128)(2,1)S(1)}, u32[]{:S(2)}, u32[]{:S(2)}) %collective-permute-start.67) | collective-permute-done | bytes 262176 | tf_op jit(solution)/shard_map/ppermute | solution.py:454
  (177 shorter events, 61.6 us)
Async XLA Ops:
  2.1 9.3 %collective-permute-start = (bf16[512,256]{1,0:T(8,128)(2,1)S(1)}, bf16[512,256]{1,0:T(8,128)(2,1)S(1)}, u32[]{:S(2)}, u32[]{:S(2)}) collective-permute-start(bf16[512,256]{1,0:T(8,128)(2,1)S(1)} %shard_map.104.refs_2_.refs_4_), channel_id=1, source_target_pairs={{0,4},{1,5},{4,8},{5,9},{8,12},{9,13},{12,14},{13,15},{14,10},{15,... | collective-permute-start | bytes 786440 | tf_op jit(solution)/shard_map/ppermute | solution.py:298
  5.1 8.0 %collective-permute-start.2 = (bf16[512,256]{1,0:T(8,128)(2,1)S(1)}, bf16[512,256]{1,0:T(8,128)(2,1)S(1)}, u32[]{:S(2)}, u32[]{:S(2)}) collective-permute-start(bf16[512,256]{1,0:T(8,128)(2,1)S(1)} %shard_map.104.refs_2_.refs_4_), channel_id=1, source_target_pairs={{4,0},{5,1},{8,4},{9,5},{12,8},{13,9},{14,12},{15,13},{10,14},{11,... | collective-permute-start | bytes 786440 | tf_op jit(solution)/shard_map/ppermute | solution.py:299
  5.1 8.8 %collective-permute-start.3 = (bf16[512,256]{1,0:T(8,128)(2,1)S(1)}, bf16[512,256]{1,0:T(8,128)(2,1)S(1)}, u32[]{:S(2)}, u32[]{:S(2)}) collective-permute-start(bf16[512,256]{1,0:T(8,128)(2,1)S(1)} %shard_map.104.refs_2_.refs_4_), channel_id=1, source_target_pairs={{0,1},{1,0},{4,5},{5,4},{8,9},{9,8},{12,13},{13,12},{14,15},{15,14... | collective-permute-start | bytes 786440 | tf_op jit(solution)/shard_map/ppermute | solution.py:300
  11.3 8.6 %collective-permute-start.1 = (bf16[512,256]{1,0:T(8,128)(2,1)S(1)}, bf16[512,256]{1,0:T(8,128)(2,1)S(1)}, u32[]{:S(2)}, u32[]{:S(2)}) collective-permute-start(bf16[512,256]{1,0:T(8,128)(2,1)S(1)} %collective-permute-done.refs_0_), channel_id=1, source_target_pairs={{0,4},{1,5},{4,8},{5,9},{8,12},{9,13},{12,14},{13,15},{14,10},{15,... | collective-permute-start | bytes 786440 | tf_op jit(solution)/shard_map/ppermute | solution.py:298
  13.2 8.6 %collective-permute-start.5 = (bf16[512,256]{1,0:T(8,128)(2,1)S(1)}, bf16[512,256]{1,0:T(8,128)(2,1)S(1)}, u32[]{:S(2)}, u32[]{:S(2)}) collective-permute-start(bf16[512,256]{1,0:T(8,128)(2,1)S(1)} %collective-permute-done.2.refs_1_), channel_id=1, source_target_pairs={{4,0},{5,1},{8,4},{9,5},{12,8},{13,9},{14,12},{15,13},{10,14},{11,... | collective-permute-start | bytes 786440 | tf_op jit(solution)/shard_map/ppermute | solution.py:299
  13.4 8.6 %collective-permute-start.6 = (bf16[512,256]{1,0:T(8,128)(2,1)S(1)}, bf16[512,256]{1,0:T(8,128)(2,1)S(1)}, u32[]{:S(2)}, u32[]{:S(2)}) collective-permute-start(bf16[512,256]{1,0:T(8,128)(2,1)S(1)} %collective-permute-done.refs_0_), channel_id=1, source_target_pairs={{0,1},{1,0},{4,5},{5,4},{8,9},{9,8},{12,13},{13,12},{14,15},{15,14... | collective-permute-start | bytes 786440 | tf_op jit(solution)/shard_map/ppermute | solution.py:300
  13.4 9.1 %collective-permute-start.7 = (bf16[512,256]{1,0:T(8,128)(2,1)S(1)}, bf16[512,256]{1,0:T(8,128)(2,1)S(1)}, u32[]{:S(2)}, u32[]{:S(2)}) collective-permute-start(bf16[512,256]{1,0:T(8,128)(2,1)S(1)} %collective-permute-done.2.refs_1_), channel_id=1, source_target_pairs={{0,1},{1,0},{4,5},{5,4},{8,9},{9,8},{12,13},{13,12},{14,15},{15,14... | collective-permute-start | bytes 786440 | tf_op jit(solution)/shard_map/ppermute | solution.py:300
  19.9 7.8 %collective-permute-start.4 = (bf16[512,256]{1,0:T(8,128)(2,1)S(1)}, bf16[512,256]{1,0:T(8,128)(2,1)S(1)}, u32[]{:S(2)}, u32[]{:S(2)}) collective-permute-start(bf16[512,256]{1,0:T(8,128)(2,1)S(1)} %collective-permute-done.1.refs_0_), channel_id=1, source_target_pairs={{0,4},{1,5},{4,8},{5,9},{8,12},{9,13},{12,14},{13,15},{14,10},{15,... | collective-permute-start | bytes 786440 | tf_op jit(solution)/shard_map/ppermute | solution.py:298
  21.7 7.8 %collective-permute-start.9 = (bf16[512,256]{1,0:T(8,128)(2,1)S(1)}, bf16[512,256]{1,0:T(8,128)(2,1)S(1)}, u32[]{:S(2)}, u32[]{:S(2)}) collective-permute-start(bf16[512,256]{1,0:T(8,128)(2,1)S(1)} %collective-permute-done.5.refs_1_), channel_id=1, source_target_pairs={{4,0},{5,1},{8,4},{9,5},{12,8},{13,9},{14,12},{15,13},{10,14},{11,... | collective-permute-start | bytes 786440 | tf_op jit(solution)/shard_map/ppermute | solution.py:299
  21.9 7.9 %collective-permute-start.11 = (bf16[512,256]{1,0:T(8,128)(2,1)S(1)}, bf16[512,256]{1,0:T(8,128)(2,1)S(1)}, u32[]{:S(2)}, u32[]{:S(2)}) collective-permute-start(bf16[512,256]{1,0:T(8,128)(2,1)S(1)} %collective-permute-done.5.refs_1_), channel_id=1, source_target_pairs={{0,1},{1,0},{4,5},{5,4},{8,9},{9,8},{12,13},{13,12},{14,15},{15,14... | collective-permute-start | bytes 786440 | tf_op jit(solution)/shard_map/ppermute | solution.py:300
  21.9 8.4 %collective-permute-start.10 = (bf16[512,256]{1,0:T(8,128)(2,1)S(1)}, bf16[512,256]{1,0:T(8,128)(2,1)S(1)}, u32[]{:S(2)}, u32[]{:S(2)}) collective-permute-start(bf16[512,256]{1,0:T(8,128)(2,1)S(1)} %collective-permute-done.1.refs_0_), channel_id=1, source_target_pairs={{0,1},{1,0},{4,5},{5,4},{8,9},{9,8},{12,13},{13,12},{14,15},{15,14... | collective-permute-start | bytes 786440 | tf_op jit(solution)/shard_map/ppermute | solution.py:300
  40.9 7.9 %collective-permute-start.20 = (bf16[512,256]{1,0:T(8,128)(2,1)S(1)}, bf16[512,256]{1,0:T(8,128)(2,1)S(1)}, u32[]{:S(2)}, u32[]{:S(2)}) collective-permute-start(bf16[512,256]{1,0:T(8,128)(2,1)S(1)} %get-tuple-element.161), channel_id=1, source_target_pairs={{0,1},{1,0},{4,5},{5,4},{8,9},{9,8},{12,13},{13,12},{14,15},{15,14... | collective-permute-start | bytes 786440 | tf_op jit(solution)/shard_map/ppermute | solution.py:300
  41.4 7.4 %collective-permute-start.22 = (bf16[512,256]{1,0:T(8,128)(2,1)S(1)}, bf16[512,256]{1,0:T(8,128)(2,1)S(1)}, u32[]{:S(2)}, u32[]{:S(2)}) collective-permute-start(bf16[512,256]{1,0:T(8,128)(2,1)S(1)} %get-tuple-element.164), channel_id=1, source_target_pairs={{0,1},{1,0},{4,5},{5,4},{8,9},{9,8},{12,13},{13,12},{14,15},{15,14... | collective-permute-start | bytes 786440 | tf_op jit(solution)/shard_map/ppermute | solution.py:300
  49.0 7.6 %collective-permute-start.21 = (bf16[512,256]{1,0:T(8,128)(2,1)S(1)}, bf16[512,256]{1,0:T(8,128)(2,1)S(1)}, u32[]{:S(2)}, u32[]{:S(2)}) collective-permute-start(bf16[512,256]{1,0:T(8,128)(2,1)S(1)} %pad_maximum_fusion), channel_id=1, source_target_pairs={{0,4},{1,5},{4,8},{5,9},{8,12},{9,13},{12,14},{13,15},{14,10},{15,... | collective-permute-start | bytes 786440 | tf_op jit(solution)/shard_map/ppermute | solution.py:298
  50.7 7.3 %collective-permute-start.26 = (bf16[512,256]{1,0:T(8,128)(2,1)S(1)}, bf16[512,256]{1,0:T(8,128)(2,1)S(1)}, u32[]{:S(2)}, u32[]{:S(2)}) collective-permute-start(bf16[512,256]{1,0:T(8,128)(2,1)S(1)} %pad_maximum_fusion.1), channel_id=1, source_target_pairs={{4,0},{5,1},{8,4},{9,5},{12,8},{13,9},{14,12},{15,13},{10,14},{11,... | collective-permute-start | bytes 786440 | tf_op jit(solution)/shard_map/ppermute | solution.py:299
  51.2 6.8 %collective-permute-start.19 = (bf16[512,256]{1,0:T(8,128)(2,1)S(1)}, bf16[512,256]{1,0:T(8,128)(2,1)S(1)}, u32[]{:S(2)}, u32[]{:S(2)}) collective-permute-start(bf16[512,256]{1,0:T(8,128)(2,1)S(1)} %get-tuple-element.159), channel_id=1, source_target_pairs={{0,1},{1,0},{4,5},{5,4},{8,9},{9,8},{12,13},{13,12},{14,15},{15,14... | collective-permute-start | bytes 786440 | tf_op jit(solution)/shard_map/ppermute | solution.py:300
  51.2 8.4 %collective-permute-start.25 = (bf16[512,256]{1,0:T(8,128)(2,1)S(1)}, bf16[512,256]{1,0:T(8,128)(2,1)S(1)}, u32[]{:S(2)}, u32[]{:S(2)}) collective-permute-start(bf16[512,256]{1,0:T(8,128)(2,1)S(1)} %get-tuple-element.166), channel_id=1, source_target_pairs={{0,1},{1,0},{4,5},{5,4},{8,9},{9,8},{12,13},{13,12},{14,15},{15,14... | collective-permute-start | bytes 786440 | tf_op jit(solution)/shard_map/ppermute | solution.py:300
  59.7 6.8 %collective-permute-start.31 = (bf16[512,256]{1,0:T(8,128)(2,1)S(1)}, bf16[512,256]{1,0:T(8,128)(2,1)S(1)}, u32[]{:S(2)}, u32[]{:S(2)}) collective-permute-start(bf16[512,256]{1,0:T(8,128)(2,1)S(1)} %add_convert_fusion.8), channel_id=1, source_target_pairs={{4,0},{5,1},{8,4},{9,5},{12,8},{13,9},{14,12},{15,13},{10,14},{11,... | collective-permute-start | bytes 786440 | tf_op jit(solution)/shard_map/ppermute | solution.py:299
  76.8 6.9 %collective-permute-start.37 = (bf16[512,256]{1,0:T(8,128)(2,1)S(1)}, bf16[512,256]{1,0:T(8,128)(2,1)S(1)}, u32[]{:S(2)}, u32[]{:S(2)}) collective-permute-start(bf16[512,256]{1,0:T(8,128)(2,1)S(1)} %get-tuple-element.187.refs_2_), channel_id=1, source_target_pairs={{0,1},{1,0},{4,5},{5,4},{8,9},{9,8},{12,13},{13,12},{14,15},{15,14... | collective-permute-start | bytes 786440 | tf_op jit(solution)/shard_map/ppermute | solution.py:300
  83.2 6.9 %collective-permute-start.41 = (bf16[512,256]{1,0:T(8,128)(2,1)S(1)}, bf16[512,256]{1,0:T(8,128)(2,1)S(1)}, u32[]{:S(2)}, u32[]{:S(2)}) collective-permute-start(bf16[512,256]{1,0:T(8,128)(2,1)S(1)} %collective-permute-done.36.refs_1_), channel_id=1, source_target_pairs={{0,1},{1,0},{4,5},{5,4},{8,9},{9,8},{12,13},{13,12},{14,15},{15,14... | collective-permute-start | bytes 786440 | tf_op jit(solution)/shard_map/ppermute | solution.py:300
  89.5 7.2 %collective-permute-start.45 = (bf16[512,256]{1,0:T(8,128)(2,1)S(1)}, bf16[512,256]{1,0:T(8,128)(2,1)S(1)}, u32[]{:S(2)}, u32[]{:S(2)}) collective-permute-start(bf16[512,256]{1,0:T(8,128)(2,1)S(1)} %collective-permute-done.39.refs_1_), channel_id=1, source_target_pairs={{0,1},{1,0},{4,5},{5,4},{8,9},{9,8},{12,13},{13,12},{14,15},{15,14... | collective-permute-start | bytes 786440 | tf_op jit(solution)/shard_map/ppermute | solution.py:300
  89.6 9.0 %collective-permute-start.44 = (bf16[512,256]{1,0:T(8,128)(2,1)S(1)}, bf16[512,256]{1,0:T(8,128)(2,1)S(1)}, u32[]{:S(2)}, u32[]{:S(2)}) collective-permute-start(bf16[512,256]{1,0:T(8,128)(2,1)S(1)} %collective-permute-done.35.refs_0_), channel_id=1, source_target_pairs={{0,1},{1,0},{4,5},{5,4},{8,9},{9,8},{12,13},{13,12},{14,15},{15,14... | collective-permute-start | bytes 786440 | tf_op jit(solution)/shard_map/ppermute | solution.py:300
  115.1 8.1 %collective-permute-start.55 = (bf16[512,256]{1,0:T(8,128)(2,1)S(1)}, bf16[512,256]{1,0:T(8,128)(2,1)S(1)}, u32[]{:S(2)}, u32[]{:S(2)}) collective-permute-start(bf16[512,256]{1,0:T(8,128)(2,1)S(1)} %pad_maximum_fusion.2), channel_id=1, source_target_pairs={{0,4},{1,5},{4,8},{5,9},{8,12},{9,13},{12,14},{13,15},{14,10},{15,... | collective-permute-start | bytes 786440 | tf_op jit(solution)/shard_map/ppermute | solution.py:298
  115.4 7.9 %collective-permute-start.60 = (bf16[512,256]{1,0:T(8,128)(2,1)S(1)}, bf16[512,256]{1,0:T(8,128)(2,1)S(1)}, u32[]{:S(2)}, u32[]{:S(2)}) collective-permute-start(bf16[512,256]{1,0:T(8,128)(2,1)S(1)} %pad_maximum_fusion.3), channel_id=1, source_target_pairs={{4,0},{5,1},{8,4},{9,5},{12,8},{13,9},{14,12},{15,13},{10,14},{11,... | collective-permute-start | bytes 786440 | tf_op jit(solution)/shard_map/ppermute | solution.py:299
  123.3 8.9 %collective-permute-start.62 = (bf16[512,256]{1,0:T(8,128)(2,1)S(1)}, bf16[512,256]{1,0:T(8,128)(2,1)S(1)}, u32[]{:S(2)}, u32[]{:S(2)}) collective-permute-start(bf16[512,256]{1,0:T(8,128)(2,1)S(1)} %get-tuple-element.233), channel_id=1, source_target_pairs={{0,1},{1,0},{4,5},{5,4},{8,9},{9,8},{12,13},{13,12},{14,15},{15,14... | collective-permute-start | bytes 786440 | tf_op jit(solution)/shard_map/ppermute | solution.py:300
  123.5 8.7 %collective-permute-start.58 = (bf16[512,256]{1,0:T(8,128)(2,1)S(1)}, bf16[512,256]{1,0:T(8,128)(2,1)S(1)}, u32[]{:S(2)}, u32[]{:S(2)}) collective-permute-start(bf16[512,256]{1,0:T(8,128)(2,1)S(1)} %add_convert_fusion.4), channel_id=1, source_target_pairs={{0,4},{1,5},{4,8},{5,9},{8,12},{9,13},{12,14},{13,15},{14,10},{15,... | collective-permute-start | bytes 786440 | tf_op jit(solution)/shard_map/ppermute | solution.py:298
  123.9 8.7 %collective-permute-start.65 = (bf16[512,256]{1,0:T(8,128)(2,1)S(1)}, bf16[512,256]{1,0:T(8,128)(2,1)S(1)}, u32[]{:S(2)}, u32[]{:S(2)}) collective-permute-start(bf16[512,256]{1,0:T(8,128)(2,1)S(1)} %add_convert_fusion.3), channel_id=1, source_target_pairs={{4,0},{5,1},{8,4},{9,5},{12,8},{13,9},{14,12},{15,13},{10,14},{11,... | collective-permute-start | bytes 786440 | tf_op jit(solution)/shard_map/ppermute | solution.py:299
  125.7 6.9 %collective-permute-start.64 = (bf16[512,256]{1,0:T(8,128)(2,1)S(1)}, bf16[512,256]{1,0:T(8,128)(2,1)S(1)}, u32[]{:S(2)}, u32[]{:S(2)}) collective-permute-start(bf16[512,256]{1,0:T(8,128)(2,1)S(1)} %get-tuple-element.234), channel_id=1, source_target_pairs={{0,1},{1,0},{4,5},{5,4},{8,9},{9,8},{12,13},{13,12},{14,15},{15,14... | collective-permute-start | bytes 786440 | tf_op jit(solution)/shard_map/ppermute | solution.py:300
  132.3 7.9 %collective-permute-start.63 = (bf16[512,256]{1,0:T(8,128)(2,1)S(1)}, bf16[512,256]{1,0:T(8,128)(2,1)S(1)}, u32[]{:S(2)}, u32[]{:S(2)}) collective-permute-start(bf16[512,256]{1,0:T(8,128)(2,1)S(1)} %add_convert_fusion.2), channel_id=1, source_target_pairs={{0,4},{1,5},{4,8},{5,9},{8,12},{9,13},{12,14},{13,15},{14,10},{15,... | collective-permute-start | bytes 786440 | tf_op jit(solution)/shard_map/ppermute | solution.py:298
  132.7 7.6 %collective-permute-start.66 = (bf16[512,256]{1,0:T(8,128)(2,1)S(1)}, bf16[512,256]{1,0:T(8,128)(2,1)S(1)}, u32[]{:S(2)}, u32[]{:S(2)}) collective-permute-start(bf16[512,256]{1,0:T(8,128)(2,1)S(1)} %add_convert_fusion.1), channel_id=1, source_target_pairs={{4,0},{5,1},{8,4},{9,5},{12,8},{13,9},{14,12},{15,13},{10,14},{11,... | collective-permute-start | bytes 786440 | tf_op jit(solution)/shard_map/ppermute | solution.py:299
  134.5 9.6 %collective-permute-start.33 = (bf16[512,256]{1,0:T(8,128)(2,1)S(1)}, bf16[512,256]{1,0:T(8,128)(2,1)S(1)}, u32[]{:S(2)}, u32[]{:S(2)}) collective-permute-start(bf16[512,256]{1,0:T(8,128)(2,1)S(1)} %get-tuple-element.186), channel_id=1, source_target_pairs={{0,16},{1,17},{2,18},{3,19},{4,20},{5,21},{6,22},{7,23},{8,24},{9,... | collective-permute-start | bytes 786440 | tf_op jit(solution)/shard_map/ppermute | solution.py:417
  140.5 8.7 %collective-permute-start.67 = (bf16[512,256]{1,0:T(8,128)(2,1)S(1)}, bf16[512,256]{1,0:T(8,128)(2,1)S(1)}, u32[]{:S(2)}, u32[]{:S(2)}) collective-permute-start(bf16[512,256]{1,0:T(8,128)(2,1)S(1)} %add_convert_fusion), channel_id=1, source_target_pairs={{16,0},{17,1},{18,2},{19,3},{20,4},{21,5},{22,6},{23,7},{24,8},{25... | collective-permute-start | bytes 786440 | tf_op jit(solution)/shard_map/ppermute | solution.py:454
  (42 other events, 235.8 us)
where the time goes:
time: 150 us
  waiting for transfers between devices  52.3 us (35%)
  starting transfers between devices  47.4 us (32%)
  Pallas kernels  44.9 us (30%)
  local copies, waits for them, and re-layouts  2.85 us (2%)
    pallas_call x27, Pallas kernels, call(): pl.pallas_call(body, out_shape=[pltpu.VMEM(shape, dtype) for shape, dtype...  44.9 us
    ppermute x16, waiting for transfers between devices, per_device(): send_fw = lambda v: lax.ppermute(v, 'dp', forward)  33.2 us
    ppermute x16, starting transfers between devices, per_device(): send_fw = lambda v: lax.ppermute(v, 'dp', forward)  23.6 us
    ppermute x16, waiting for transfers between devices, per_device(): send_bw = lambda v: lax.ppermute(v, 'dp', backward)  12.5 us
    ppermute x16, starting transfers between devices, per_device(): send_bw = lambda v: lax.ppermute(v, 'dp', backward)  12 us
    ppermute x34, starting transfers between devices, per_device(): swap = lambda v: lax.ppermute(v, 'dp', sibling)  7.03 us
    ppermute x1, waiting for transfers between devices, per_device(): lax.ppermute(total.astype(bf16), 'section', [(s + 1, s) for s in range(se...  4.19 us
    ppermute x1, starting transfers between devices, per_device(): lax.ppermute(emitted, 'section', [(s, s + 1) for s in range(sections - 1)])  3.43 us
  transfers between devices with their start and end apart: 68, of which 27 were waited for; matrix products, arithmetic and copies ran while one was open for 1% of the time, Pallas kernels for 26%

commit v1 on v0

--- a/solution.py
+++ b/solution.py
@@ -305,7 +305,7 @@
     gate_hbm, up_hbm, down_hbm = gate_weight[0], up_weight[0], down_weight[0]
     spots = lambda at: [(d % chips) * 2 + s for d, s in at]
 
-    def gathered(mine, take, beside):
+    def gathered(mine, take, beside, early):
         held, own, sib = None, [], []
         fw = bw = mine
 
@@ -327,6 +327,8 @@
             else:
                 own = [(fw, (1 - k, False)), (bw, (k - 1, False))]
                 held, sib = taken(own + sib), swapped(own)
+                if k == far and early:
+                    held, sib = taken(sib), []
             fw, bw = next_fw, next_bw
             fw, held, _ = lax.optimization_barrier((fw, held, beside.get(k)))
             bw = tied(bw, held)
@@ -361,9 +363,10 @@
             a, b = sums(now_own, now_sib)
             if k == 1:
                 fw = jnp.concatenate([a[:half] + fw.astype(f32), a[half:]], axis=0).astype(bf16)
-                bw = jnp.concatenate([b[:half], b[half:] + bw.astype(f32)], axis=0).astype(bf16)
+                bw = jnp.concatenate([b[:half], b[half:] + tied(bw, fw).astype(f32)], axis=0).astype(bf16)
             else:
-                fw, bw = (a + fw.astype(f32)).astype(bf16), (b + bw.astype(f32)).astype(bf16)
+                fw = (a + fw.astype(f32)).astype(bf16)
+                bw = (b + tied(bw, fw).astype(f32)).astype(bf16)
             now_own, now_sib = later[: len(later) // 2], later[len(later) // 2 :]
         ends = [(send_fw(fw[c]), send_bw(bw[c])) for c in cut]
         return now_own[0], swap(now_sib[0]), [e[0] for e in ends], [e[1] for e in ends], cut
@@ -396,7 +399,7 @@
             down_w = new[0]
         return res
 
-    gate, upward, spikes = gathered(x, take_inputs, {1: (gate_w, up_w)})
+    gate, upward, spikes = gathered(x, take_inputs, {1: (gate_w, up_w)}, False)
 
     def blocks(kernel, flops, *args):
         def blocks_of(at, after):
@@ -442,7 +445,7 @@
             aliases=aliases,
         )[0]
 
-    gate_grad, up_grad = gathered(grad16, take_grads, {1: way_back})
+    gate_grad, up_grad = gathered(grad16, take_grads, {1: way_back}, True)
 
     own, sib, fw, bw, cut = scattered(
         blocks(input_grad_kernel, 4 * rows * hid * local, gate_grad, up_grad, gate_w, up_w), 1

time: 150 us -> 148 us (0.987)
  waiting for transfers between devices: 52.3 us -> 48.7 us
    ppermute x16, waiting for transfers between devices: 33.2 us -> 28.6 us  [per_device(): send_fw = lambda v: lax.ppermute(v, 'dp', forward)]
    pallas_call x27 -> x28, Pallas kernels: 44.9 us -> 45.3 us  [call(): pl.pallas_call(body, out_shape=[pltpu.VMEM(shape, dtype) for shape, dtype...]
  transfers between devices with their start and end apart: 68 -> 68, of which waited for: 27 -> 28; matrix products, arithmetic and copies ran while one was open for 1% -> 1% of each run, Pallas kernels for 26% -> 27%
where the time goes in v1:
time: 148 us; the launch traced here: 147 us
  waiting for transfers between devices  48.7 us (33%)
  starting transfers between devices  48 us (32%)
  Pallas kernels  45.3 us (31%)
  local copies, waits for them, and re-layouts  2.85 us (2%)
    pallas_call x28, Pallas kernels, call(): pl.pallas_call(body, out_shape=[pltpu.VMEM(shape, dtype) for shape, dtype...  45.3 us
    ppermute x16, waiting for transfers between devices, per_device(): send_fw = lambda v: lax.ppermute(v, 'dp', forward)  28.6 us
    ppermute x16, starting transfers between devices, per_device(): send_fw = lambda v: lax.ppermute(v, 'dp', forward)  24.3 us
    ppermute x16, waiting for transfers between devices, per_device(): send_bw = lambda v: lax.ppermute(v, 'dp', backward)  13.6 us
    ppermute x16, starting transfers between devices, per_device(): send_bw = lambda v: lax.ppermute(v, 'dp', backward)  11.3 us
    ppermute x34, starting transfers between devices, per_device(): swap = lambda v: lax.ppermute(v, 'dp', sibling)  7.79 us
    ppermute x1, waiting for transfers between devices, per_device(): lax.ppermute(total.astype(bf16), 'section', [(s + 1, s) for s in range(se...  3.98 us
    ppermute x1, starting transfers between devices, per_device(): lax.ppermute(emitted, 'section', [(s, s + 1) for s in range(sections - 1)])  3.44 us
  transfers between devices with their start and end apart: 68, of which 28 were waited for; matrix products, arithmetic and copies ran while one was open for 1% of the time, Pallas kernels for 27%

profile of v1, /device:TPU:0, one launch (start us, length us, event | category | flops | bytes accessed | tf_op | source)
XLA Modules:
  0.0 147.5 jit_solution(3423079882563500680)
XLA Ops:
  2.1 3.1 %collective-permute-start = (bf16[512,256]{1,0:T(8,128)(2,1)S(1)}, bf16[512,256]{1,0:T(8,128)(2,1)S(1)}, u32[]{:S(2)}, u32[]{:S(2)}) collective-permute-start(bf16[512,256]{1,0:T(8,128)(2,1)S(1)} %shard_map.104.refs_2_.refs_4_), channel_id=1, source_target_pairs={{0,4},{1,5},{4,8},{5,9},{8,12},{9,13},{12,14},{13,15},{14,10},{15,... | collective-permute-start | bytes 786440 | tf_op jit(solution)/shard_map/ppermute | solution.py:298
  5.1 5.8 %shard_map.105 = (bf16[4096,1024]{1,0:T(8,128)(2,1)S(1)}, bf16[4096,1024]{1,0:T(8,128)(2,1)S(1)}) custom-call(bf16[4096,1024]{1,0:T(8,128)(2,1)} %bitcast.16, bf16[4096,1024]{1,0:T(8,128)(2,1)} %bitcast.17), custom_call_target="tpu_custom_call" | custom-call | flops 1 | bytes 1 | tf_op jit(solution)/shard_map/pallas_call | solution.py:49
  11.3 1.8 %collective-permute-start.1 = (bf16[512,256]{1,0:T(8,128)(2,1)S(1)}, bf16[512,256]{1,0:T(8,128)(2,1)S(1)}, u32[]{:S(2)}, u32[]{:S(2)}) collective-permute-start(bf16[512,256]{1,0:T(8,128)(2,1)S(1)} %collective-permute-done.refs_0_), channel_id=1, source_target_pairs={{0,4},{1,5},{4,8},{5,9},{8,12},{9,13},{12,14},{13,15},{14,10},{15,... | collective-permute-start | bytes 786440 | tf_op jit(solution)/shard_map/ppermute | solution.py:298
  13.9 3.4 %shard_map.106 = (f32[512,1024]{1,0:T(8,128)S(1)}, f32[512,1024]{1,0:T(8,128)S(1)}, bf16[1024,4096]{1,0:T(8,128)(2,1)S(1)}) custom-call(bf16[512,256]{1,0:T(8,128)(2,1)S(1)} %collective-permute-done.refs_0_, bf16[512,256]{1,0:T(8,128)(2,1)S(1)} %collective-permute-done.2.refs_1_, bf16[512,256]{1,0:T(8,128)(2,1)S(1)} %shard_map.104.refs_2_.refs_4_, ...), custom_call_target="tpu_custom_call" | custom-call | flops 1 | bytes 1 | tf_op jit(solution)/shard_map/pallas_call | solution.py:49
  17.3 2.6 %collective-permute-done.1.refs_0_ = bf16[512,256]{1,0:T(8,128)(2,1)S(1)} collective-permute-done((bf16[512,256]{1,0:T(8,128)(2,1)S(1)}, bf16[512,256]{1,0:T(8,128)(2,1)S(1)}, u32[]{:S(2)}, u32[]{:S(2)}) %collective-permute-start.1) | collective-permute-done | bytes 262176 | tf_op jit(solution)/shard_map/ppermute | solution.py:298
  19.9 1.8 %collective-permute-start.4 = (bf16[512,256]{1,0:T(8,128)(2,1)S(1)}, bf16[512,256]{1,0:T(8,128)(2,1)S(1)}, u32[]{:S(2)}, u32[]{:S(2)}) collective-permute-start(bf16[512,256]{1,0:T(8,128)(2,1)S(1)} %collective-permute-done.1.refs_0_), channel_id=1, source_target_pairs={{0,4},{1,5},{4,8},{5,9},{8,12},{9,13},{12,14},{13,15},{14,10},{15,... | collective-permute-start | bytes 786440 | tf_op jit(solution)/shard_map/ppermute | solution.py:298
  22.5 2.8 %shard_map.107 = (f32[512,1024]{1,0:T(8,128)S(1)}, f32[512,1024]{1,0:T(8,128)S(1)}) custom-call(bf16[512,256]{1,0:T(8,128)(2,1)S(1)} %collective-permute-done.1.refs_0_, bf16[512,256]{1,0:T(8,128)(2,1)S(1)} %collective-permute-done.5.refs_1_, bf16[512,256]{1,0:T(8,128)(2,1)S(1)} %collective-permute-done.6.refs_2_, ...), custom_call_target="tpu_custom_call", output_to_operand_aliasing={{0}: (6, {}), {1}: (7, {})} | custom-call | flops 1 | bytes 1 | tf_op jit(solution)/shard_map/pallas_call | solution.py:49
  25.2 2.5 %collective-permute-done.4.refs_0_ = bf16[512,256]{1,0:T(8,128)(2,1)S(1)} collective-permute-done((bf16[512,256]{1,0:T(8,128)(2,1)S(1)}, bf16[512,256]{1,0:T(8,128)(2,1)S(1)}, u32[]{:S(2)}, u32[]{:S(2)}) %collective-permute-start.4) | collective-permute-done | bytes 262176 | tf_op jit(solution)/shard_map/ppermute | solution.py:298
  27.7 1.9 %collective-permute-start.8 = (bf16[256,256]{1,0:T(8,128)(2,1)S(1)}, bf16[256,256]{1,0:T(8,128)(2,1)S(1)}, u32[]{:S(2)}, u32[]{:S(2)}) collective-permute-start(bf16[256,256]{1,0:T(8,128)(2,1)S(1)} %slice.56), channel_id=1, source_target_pairs={{0,4},{1,5},{4,8},{5,9},{8,12},{9,13},{12,14},{13,15},{14,10},{15,... | collective-permute-start | bytes 393224 | tf_op jit(solution)/shard_map/ppermute | solution.py:298
  30.3 2.8 %shard_map.108 = (f32[512,1024]{1,0:T(8,128)S(1)}, f32[512,1024]{1,0:T(8,128)S(1)}) custom-call(bf16[512,256]{1,0:T(8,128)(2,1)S(1)} %collective-permute-done.4.refs_0_, bf16[512,256]{1,0:T(8,128)(2,1)S(1)} %collective-permute-done.9.refs_1_, bf16[512,256]{1,0:T(8,128)(2,1)S(1)} %collective-permute-done.10.refs_2_, ...), custom_call_target="tpu_custom_call", output_to_operand_aliasing={{0}: (6, {}), {1}: (7, {})} | custom-call | flops 1 | bytes 1 | tf_op jit(solution)/shard_map/pallas_call | solution.py:49
  35.1 2.2 %shard_map.109 = (f32[512,1024]{1,0:T(8,128)S(1)}, f32[512,1024]{1,0:T(8,128)S(1)}) custom-call(bf16[256,256]{1,0:T(8,128)(2,1)S(1)} %collective-permute-done.8.refs_0_, bf16[256,256]{1,0:T(8,128)(2,1)S(1)} %collective-permute-done.13.refs_1_, bf16[512,256]{1,0:T(8,128)(2,1)S(1)} %collective-permute-done.15.refs_2_, ...), custom_call_target="tpu_custom_call", output_to_operand_aliasing={{0}: (6, {}), {1}: (7, {})} | custom-call | flops 1 | bytes 1 | tf_op jit(solution)/shard_map/pallas_call | solution.py:49
  37.4 1.9 %shard_map.110 = (f32[512,1024]{1,0:T(8,128)S(1)}, f32[512,1024]{1,0:T(8,128)S(1)}, bf16[512,1024]{1,0:T(8,128)(2,1)S(1)}) custom-call(bf16[256,256]{1,0:T(8,128)(2,1)S(1)} %collective-permute-done.12.refs_0_, bf16[256,256]{1,0:T(8,128)(2,1)S(1)} %collective-permute-done.14.refs_1_, ...), custom_call_target="tpu_custom_call", output_to_operand_aliasing={{0}: (4, {}), {1}: (5, {})} | custom-call | flops 1 | bytes 1 | tf_op jit(solution)/shard_map/pallas_call | solution.py:49
  53.0 3.6 %collective-permute-done.21 = bf16[512,256]{1,0:T(8,128)(2,1)S(1)} collective-permute-done((bf16[512,256]{1,0:T(8,128)(2,1)S(1)}, bf16[512,256]{1,0:T(8,128)(2,1)S(1)}, u32[]{:S(2)}, u32[]{:S(2)}) %collective-permute-start.21) | collective-permute-done | bytes 262176 | tf_op jit(solution)/shard_map/ppermute | solution.py:298
  61.8 2.8 %collective-permute-done.24 = bf16[512,256]{1,0:T(8,128)(2,1)S(1)} collective-permute-done((bf16[512,256]{1,0:T(8,128)(2,1)S(1)}, bf16[512,256]{1,0:T(8,128)(2,1)S(1)}, u32[]{:S(2)}, u32[]{:S(2)}) %collective-permute-start.24) | collective-permute-done | bytes 262176 | tf_op jit(solution)/shard_map/ppermute | solution.py:298
  64.5 1.9 %collective-permute-done.31 = bf16[512,256]{1,0:T(8,128)(2,1)S(1)} collective-permute-done((bf16[512,256]{1,0:T(8,128)(2,1)S(1)}, bf16[512,256]{1,0:T(8,128)(2,1)S(1)}, u32[]{:S(2)}, u32[]{:S(2)}) %collective-permute-start.31) | collective-permute-done | bytes 262176 | tf_op jit(solution)/shard_map/ppermute | solution.py:299
  69.2 3.9 %collective-permute-done.32.refs_3_ = bf16[512,256]{1,0:T(8,128)(2,1)S(1)} collective-permute-done((bf16[512,256]{1,0:T(8,128)(2,1)S(1)}, bf16[512,256]{1,0:T(8,128)(2,1)S(1)}, u32[]{:S(2)}, u32[]{:S(2)}) %collective-permute-start.32) | collective-permute-done | bytes 262176 | tf_op jit(solution)/shard_map/ppermute | solution.py:299
  74.1 2.5 %collective-permute-start.34 = (bf16[512,256]{1,0:T(8,128)(2,1)S(1)}, bf16[512,256]{1,0:T(8,128)(2,1)S(1)}, u32[]{:S(2)}, u32[]{:S(2)}) collective-permute-start(bf16[512,256]{1,0:T(8,128)(2,1)S(1)} %get-tuple-element.196.refs_2_), channel_id=1, source_target_pairs={{0,4},{1,5},{4,8},{5,9},{8,12},{9,13},{12,14},{13,15},{14,10},{15,... | collective-permute-start | bytes 786440 | tf_op jit(solution)/shard_map/ppermute | solution.py:298
  76.6 1.8 %shard_map.119 = (f32[512,1024]{1,0:T(8,128)S(1)}, f32[512,1024]{1,0:T(8,128)S(1)}, f32[512,1024]{1,0:T(8,128)S(1)}) custom-call(f32[512,1024]{1,0:T(8,128)S(1)} %get-tuple-element.198.refs_0_, f32[512,1024]{1,0:T(8,128)S(1)} %get-tuple-element.199.refs_1_, s32[1,1024]{1,0:T(1,128)S(1)} %copy-done.2, s32[1,1024]{1,0:T(1,128)S(1)} %copy-done.3), custom_call_target="tpu_custom_call" | custom-call | flops 268435456 | bytes 524288 | tf_op jit(solution)/shard_map/pallas_call | solution.py:49
  78.4 2.1 %collective-permute-done.34.refs_0_ = bf16[512,256]{1,0:T(8,128)(2,1)S(1)} collective-permute-done((bf16[512,256]{1,0:T(8,128)(2,1)S(1)}, bf16[512,256]{1,0:T(8,128)(2,1)S(1)}, u32[]{:S(2)}, u32[]{:S(2)}) %collective-permute-start.34) | collective-permute-done | bytes 262176 | tf_op jit(solution)/shard_map/ppermute | solution.py:298
  80.5 2.5 %collective-permute-start.35 = (bf16[512,256]{1,0:T(8,128)(2,1)S(1)}, bf16[512,256]{1,0:T(8,128)(2,1)S(1)}, u32[]{:S(2)}, u32[]{:S(2)}) collective-permute-start(bf16[512,256]{1,0:T(8,128)(2,1)S(1)} %collective-permute-done.34.refs_0_), channel_id=1, source_target_pairs={{0,4},{1,5},{4,8},{5,9},{8,12},{9,13},{12,14},{13,15},{14,10},{15,... | collective-permute-start | bytes 786440 | tf_op jit(solution)/shard_map/ppermute | solution.py:298
  85.0 2.2 %collective-permute-done.35.refs_0_ = bf16[512,256]{1,0:T(8,128)(2,1)S(1)} collective-permute-done((bf16[512,256]{1,0:T(8,128)(2,1)S(1)}, bf16[512,256]{1,0:T(8,128)(2,1)S(1)}, u32[]{:S(2)}, u32[]{:S(2)}) %collective-permute-start.35) | collective-permute-done | bytes 262176 | tf_op jit(solution)/shard_map/ppermute | solution.py:298
  87.2 2.1 %collective-permute-start.38 = (bf16[512,256]{1,0:T(8,128)(2,1)S(1)}, bf16[512,256]{1,0:T(8,128)(2,1)S(1)}, u32[]{:S(2)}, u32[]{:S(2)}) collective-permute-start(bf16[512,256]{1,0:T(8,128)(2,1)S(1)} %collective-permute-done.35.refs_0_), channel_id=1, source_target_pairs={{0,4},{1,5},{4,8},{5,9},{8,12},{9,13},{12,14},{13,15},{14,10},{15,... | collective-permute-start | bytes 786440 | tf_op jit(solution)/shard_map/ppermute | solution.py:298
  91.5 2.1 %collective-permute-done.38.refs_0_ = bf16[512,256]{1,0:T(8,128)(2,1)S(1)} collective-permute-done((bf16[512,256]{1,0:T(8,128)(2,1)S(1)}, bf16[512,256]{1,0:T(8,128)(2,1)S(1)}, u32[]{:S(2)}, u32[]{:S(2)}) %collective-permute-start.38) | collective-permute-done | bytes 262176 | tf_op jit(solution)/shard_map/ppermute | solution.py:298
  93.6 2.1 %collective-permute-done.44.refs_1_ = bf16[512,256]{1,0:T(8,128)(2,1)S(1)} collective-permute-done((bf16[512,256]{1,0:T(8,128)(2,1)S(1)}, bf16[512,256]{1,0:T(8,128)(2,1)S(1)}, u32[]{:S(2)}, u32[]{:S(2)}) %collective-permute-start.44) | collective-permute-done | bytes 262176 | tf_op jit(solution)/shard_map/ppermute | solution.py:299
  105.8 1.8 %shard_map.126 = (f32[512,256]{1,0:T(8,128)S(1)}, bf16[512,256]{1,0:T(8,128)(2,1)S(1)}, bf16[512,256]{1,0:T(8,128)(2,1)S(1)}) custom-call(bf16[512,1024]{1,0:T(8,128)(2,1)S(1)} %get-tuple-element.247.refs_0_, bf16[512,1024]{1,0:T(8,128)(2,1)S(1)} %get-tuple-element.214.refs_1_, bf16[4096,1024]{1,0:T(8,128)(2,1)S(1)} %get-tuple-element.130.refs_4_.refs_2_, ...), custom_call_target="tpu_custom_call" | custom-call | flops 1610612736 | bytes 3145728 | tf_op jit(solution)/shard_map/pallas_call | solution.py:49
  110.4 2.4 %shard_map.129 = (f32[512,256]{1,0:T(8,128)S(1)}, f32[512,256]{1,0:T(8,128)S(1)}, bf16[512,256]{1,0:T(8,128)(2,1)S(1)}, bf16[512,256]{1,0:T(8,128)(2,1)S(1)}) custom-call(bf16[512,1024]{1,0:T(8,128)(2,1)S(1)} %get-tuple-element.247.refs_0_, bf16[512,1024]{1,0:T(8,128)(2,1)S(1)} %get-tuple-element.214.refs_1_, ...), custom_call_target="tpu_custom_call" | custom-call | flops 2147483648 | bytes 4194304 | tf_op jit(solution)/shard_map/pallas_call | solution.py:49
  117.1 2.4 %shard_map.130 = (f32[512,256]{1,0:T(8,128)S(1)}, f32[512,256]{1,0:T(8,128)S(1)}, bf16[512,256]{1,0:T(8,128)(2,1)S(1)}, bf16[512,256]{1,0:T(8,128)(2,1)S(1)}) custom-call(bf16[512,1024]{1,0:T(8,128)(2,1)S(1)} %get-tuple-element.247.refs_0_, bf16[512,1024]{1,0:T(8,128)(2,1)S(1)} %get-tuple-element.214.refs_1_, ...), custom_call_target="tpu_custom_call" | custom-call | flops 2147483648 | bytes 4194304 | tf_op jit(solution)/shard_map/pallas_call | solution.py:49
  119.5 2.9 %collective-permute-done.55 = bf16[512,256]{1,0:T(8,128)(2,1)S(1)} collective-permute-done((bf16[512,256]{1,0:T(8,128)(2,1)S(1)}, bf16[512,256]{1,0:T(8,128)(2,1)S(1)}, u32[]{:S(2)}, u32[]{:S(2)}) %collective-permute-start.55) | collective-permute-done | bytes 262176 | tf_op jit(solution)/shard_map/ppermute | solution.py:298
  126.8 2.8 %collective-permute-done.58 = bf16[512,256]{1,0:T(8,128)(2,1)S(1)} collective-permute-done((bf16[512,256]{1,0:T(8,128)(2,1)S(1)}, bf16[512,256]{1,0:T(8,128)(2,1)S(1)}, u32[]{:S(2)}, u32[]{:S(2)}) %collective-permute-start.58) | collective-permute-done | bytes 262176 | tf_op jit(solution)/shard_map/ppermute | solution.py:298
  132.1 3.4 %collective-permute-start.33 = (bf16[512,256]{1,0:T(8,128)(2,1)S(1)}, bf16[512,256]{1,0:T(8,128)(2,1)S(1)}, u32[]{:S(2)}, u32[]{:S(2)}) collective-permute-start(bf16[512,256]{1,0:T(8,128)(2,1)S(1)} %get-tuple-element.195), channel_id=1, source_target_pairs={{0,16},{1,17},{2,18},{3,19},{4,20},{5,21},{6,22},{7,23},{8,24},{9,... | collective-permute-start | bytes 786440 | tf_op jit(solution)/shard_map/ppermute | solution.py:420
  139.6 2.1 %collective-permute-done.33 = bf16[512,256]{1,0:T(8,128)(2,1)S(1)} collective-permute-done((bf16[512,256]{1,0:T(8,128)(2,1)S(1)}, bf16[512,256]{1,0:T(8,128)(2,1)S(1)}, u32[]{:S(2)}, u32[]{:S(2)}) %collective-permute-start.33) | collective-permute-done | bytes 262176 | tf_op jit(solution)/shard_map/ppermute | solution.py:420
  142.6 4.0 %collective-permute-done.67 = bf16[512,256]{1,0:T(8,128)(2,1)S(1)} collective-permute-done((bf16[512,256]{1,0:T(8,128)(2,1)S(1)}, bf16[512,256]{1,0:T(8,128)(2,1)S(1)}, u32[]{:S(2)}, u32[]{:S(2)}) %collective-permute-start.67) | collective-permute-done | bytes 262176 | tf_op jit(solution)/shard_map/ppermute | solution.py:457
  (178 shorter events, 62.4 us)
Async XLA Ops:
  2.1 9.3 %collective-permute-start = (bf16[512,256]{1,0:T(8,128)(2,1)S(1)}, bf16[512,256]{1,0:T(8,128)(2,1)S(1)}, u32[]{:S(2)}, u32[]{:S(2)}) collective-permute-start(bf16[512,256]{1,0:T(8,128)(2,1)S(1)} %shard_map.104.refs_2_.refs_4_), channel_id=1, source_target_pairs={{0,4},{1,5},{4,8},{5,9},{8,12},{9,13},{12,14},{13,15},{14,10},{15,... | collective-permute-start | bytes 786440 | tf_op jit(solution)/shard_map/ppermute | solution.py:298
  5.1 8.0 %collective-permute-start.2 = (bf16[512,256]{1,0:T(8,128)(2,1)S(1)}, bf16[512,256]{1,0:T(8,128)(2,1)S(1)}, u32[]{:S(2)}, u32[]{:S(2)}) collective-permute-start(bf16[512,256]{1,0:T(8,128)(2,1)S(1)} %shard_map.104.refs_2_.refs_4_), channel_id=1, source_target_pairs={{4,0},{5,1},{8,4},{9,5},{12,8},{13,9},{14,12},{15,13},{10,14},{11,... | collective-permute-start | bytes 786440 | tf_op jit(solution)/shard_map/ppermute | solution.py:299
  5.1 8.8 %collective-permute-start.3 = (bf16[512,256]{1,0:T(8,128)(2,1)S(1)}, bf16[512,256]{1,0:T(8,128)(2,1)S(1)}, u32[]{:S(2)}, u32[]{:S(2)}) collective-permute-start(bf16[512,256]{1,0:T(8,128)(2,1)S(1)} %shard_map.104.refs_2_.refs_4_), channel_id=1, source_target_pairs={{0,1},{1,0},{4,5},{5,4},{8,9},{9,8},{12,13},{13,12},{14,15},{15,14... | collective-permute-start | bytes 786440 | tf_op jit(solution)/shard_map/ppermute | solution.py:300
  11.3 8.6 %collective-permute-start.1 = (bf16[512,256]{1,0:T(8,128)(2,1)S(1)}, bf16[512,256]{1,0:T(8,128)(2,1)S(1)}, u32[]{:S(2)}, u32[]{:S(2)}) collective-permute-start(bf16[512,256]{1,0:T(8,128)(2,1)S(1)} %collective-permute-done.refs_0_), channel_id=1, source_target_pairs={{0,4},{1,5},{4,8},{5,9},{8,12},{9,13},{12,14},{13,15},{14,10},{15,... | collective-permute-start | bytes 786440 | tf_op jit(solution)/shard_map/ppermute | solution.py:298
  13.2 8.6 %collective-permute-start.5 = (bf16[512,256]{1,0:T(8,128)(2,1)S(1)}, bf16[512,256]{1,0:T(8,128)(2,1)S(1)}, u32[]{:S(2)}, u32[]{:S(2)}) collective-permute-start(bf16[512,256]{1,0:T(8,128)(2,1)S(1)} %collective-permute-done.2.refs_1_), channel_id=1, source_target_pairs={{4,0},{5,1},{8,4},{9,5},{12,8},{13,9},{14,12},{15,13},{10,14},{11,... | collective-permute-start | bytes 786440 | tf_op jit(solution)/shard_map/ppermute | solution.py:299
  13.4 8.6 %collective-permute-start.6 = (bf16[512,256]{1,0:T(8,128)(2,1)S(1)}, bf16[512,256]{1,0:T(8,128)(2,1)S(1)}, u32[]{:S(2)}, u32[]{:S(2)}) collective-permute-start(bf16[512,256]{1,0:T(8,128)(2,1)S(1)} %collective-permute-done.refs_0_), channel_id=1, source_target_pairs={{0,1},{1,0},{4,5},{5,4},{8,9},{9,8},{12,13},{13,12},{14,15},{15,14... | collective-permute-start | bytes 786440 | tf_op jit(solution)/shard_map/ppermute | solution.py:300
  13.4 9.1 %collective-permute-start.7 = (bf16[512,256]{1,0:T(8,128)(2,1)S(1)}, bf16[512,256]{1,0:T(8,128)(2,1)S(1)}, u32[]{:S(2)}, u32[]{:S(2)}) collective-permute-start(bf16[512,256]{1,0:T(8,128)(2,1)S(1)} %collective-permute-done.2.refs_1_), channel_id=1, source_target_pairs={{0,1},{1,0},{4,5},{5,4},{8,9},{9,8},{12,13},{13,12},{14,15},{15,14... | collective-permute-start | bytes 786440 | tf_op jit(solution)/shard_map/ppermute | solution.py:300
  19.9 7.8 %collective-permute-start.4 = (bf16[512,256]{1,0:T(8,128)(2,1)S(1)}, bf16[512,256]{1,0:T(8,128)(2,1)S(1)}, u32[]{:S(2)}, u32[]{:S(2)}) collective-permute-start(bf16[512,256]{1,0:T(8,128)(2,1)S(1)} %collective-permute-done.1.refs_0_), channel_id=1, source_target_pairs={{0,4},{1,5},{4,8},{5,9},{8,12},{9,13},{12,14},{13,15},{14,10},{15,... | collective-permute-start | bytes 786440 | tf_op jit(solution)/shard_map/ppermute | solution.py:298
  21.7 7.8 %collective-permute-start.9 = (bf16[512,256]{1,0:T(8,128)(2,1)S(1)}, bf16[512,256]{1,0:T(8,128)(2,1)S(1)}, u32[]{:S(2)}, u32[]{:S(2)}) collective-permute-start(bf16[512,256]{1,0:T(8,128)(2,1)S(1)} %collective-permute-done.5.refs_1_), channel_id=1, source_target_pairs={{4,0},{5,1},{8,4},{9,5},{12,8},{13,9},{14,12},{15,13},{10,14},{11,... | collective-permute-start | bytes 786440 | tf_op jit(solution)/shard_map/ppermute | solution.py:299
  21.9 7.9 %collective-permute-start.11 = (bf16[512,256]{1,0:T(8,128)(2,1)S(1)}, bf16[512,256]{1,0:T(8,128)(2,1)S(1)}, u32[]{:S(2)}, u32[]{:S(2)}) collective-permute-start(bf16[512,256]{1,0:T(8,128)(2,1)S(1)} %collective-permute-done.5.refs_1_), channel_id=1, source_target_pairs={{0,1},{1,0},{4,5},{5,4},{8,9},{9,8},{12,13},{13,12},{14,15},{15,14... | collective-permute-start | bytes 786440 | tf_op jit(solution)/shard_map/ppermute | solution.py:300
  21.9 8.4 %collective-permute-start.10 = (bf16[512,256]{1,0:T(8,128)(2,1)S(1)}, bf16[512,256]{1,0:T(8,128)(2,1)S(1)}, u32[]{:S(2)}, u32[]{:S(2)}) collective-permute-start(bf16[512,256]{1,0:T(8,128)(2,1)S(1)} %collective-permute-done.1.refs_0_), channel_id=1, source_target_pairs={{0,1},{1,0},{4,5},{5,4},{8,9},{9,8},{12,13},{13,12},{14,15},{15,14... | collective-permute-start | bytes 786440 | tf_op jit(solution)/shard_map/ppermute | solution.py:300
  40.9 7.9 %collective-permute-start.20 = (bf16[512,256]{1,0:T(8,128)(2,1)S(1)}, bf16[512,256]{1,0:T(8,128)(2,1)S(1)}, u32[]{:S(2)}, u32[]{:S(2)}) collective-permute-start(bf16[512,256]{1,0:T(8,128)(2,1)S(1)} %get-tuple-element.167), channel_id=1, source_target_pairs={{0,1},{1,0},{4,5},{5,4},{8,9},{9,8},{12,13},{13,12},{14,15},{15,14... | collective-permute-start | bytes 786440 | tf_op jit(solution)/shard_map/ppermute | solution.py:300
  41.4 7.4 %collective-permute-start.22 = (bf16[512,256]{1,0:T(8,128)(2,1)S(1)}, bf16[512,256]{1,0:T(8,128)(2,1)S(1)}, u32[]{:S(2)}, u32[]{:S(2)}) collective-permute-start(bf16[512,256]{1,0:T(8,128)(2,1)S(1)} %get-tuple-element.170), channel_id=1, source_target_pairs={{0,1},{1,0},{4,5},{5,4},{8,9},{9,8},{12,13},{13,12},{14,15},{15,14... | collective-permute-start | bytes 786440 | tf_op jit(solution)/shard_map/ppermute | solution.py:300
  49.0 7.6 %collective-permute-start.21 = (bf16[512,256]{1,0:T(8,128)(2,1)S(1)}, bf16[512,256]{1,0:T(8,128)(2,1)S(1)}, u32[]{:S(2)}, u32[]{:S(2)}) collective-permute-start(bf16[512,256]{1,0:T(8,128)(2,1)S(1)} %pad_maximum_fusion), channel_id=1, source_target_pairs={{0,4},{1,5},{4,8},{5,9},{8,12},{9,13},{12,14},{13,15},{14,10},{15,... | collective-permute-start | bytes 786440 | tf_op jit(solution)/shard_map/ppermute | solution.py:298
  50.7 7.3 %collective-permute-start.26 = (bf16[512,256]{1,0:T(8,128)(2,1)S(1)}, bf16[512,256]{1,0:T(8,128)(2,1)S(1)}, u32[]{:S(2)}, u32[]{:S(2)}) collective-permute-start(bf16[512,256]{1,0:T(8,128)(2,1)S(1)} %pad_maximum_fusion.1), channel_id=1, source_target_pairs={{4,0},{5,1},{8,4},{9,5},{12,8},{13,9},{14,12},{15,13},{10,14},{11,... | collective-permute-start | bytes 786440 | tf_op jit(solution)/shard_map/ppermute | solution.py:299
  51.2 6.8 %collective-permute-start.19 = (bf16[512,256]{1,0:T(8,128)(2,1)S(1)}, bf16[512,256]{1,0:T(8,128)(2,1)S(1)}, u32[]{:S(2)}, u32[]{:S(2)}) collective-permute-start(bf16[512,256]{1,0:T(8,128)(2,1)S(1)} %get-tuple-element.165), channel_id=1, source_target_pairs={{0,1},{1,0},{4,5},{5,4},{8,9},{9,8},{12,13},{13,12},{14,15},{15,14... | collective-permute-start | bytes 786440 | tf_op jit(solution)/shard_map/ppermute | solution.py:300
  51.2 8.5 %collective-permute-start.25 = (bf16[512,256]{1,0:T(8,128)(2,1)S(1)}, bf16[512,256]{1,0:T(8,128)(2,1)S(1)}, u32[]{:S(2)}, u32[]{:S(2)}) collective-permute-start(bf16[512,256]{1,0:T(8,128)(2,1)S(1)} %get-tuple-element.172), channel_id=1, source_target_pairs={{0,1},{1,0},{4,5},{5,4},{8,9},{9,8},{12,13},{13,12},{14,15},{15,14... | collective-permute-start | bytes 786440 | tf_op jit(solution)/shard_map/ppermute | solution.py:300
  59.7 6.7 %collective-permute-start.31 = (bf16[512,256]{1,0:T(8,128)(2,1)S(1)}, bf16[512,256]{1,0:T(8,128)(2,1)S(1)}, u32[]{:S(2)}, u32[]{:S(2)}) collective-permute-start(bf16[512,256]{1,0:T(8,128)(2,1)S(1)} %add_convert_fusion.8), channel_id=1, source_target_pairs={{4,0},{5,1},{8,4},{9,5},{12,8},{13,9},{14,12},{15,13},{10,14},{11,... | collective-permute-start | bytes 786440 | tf_op jit(solution)/shard_map/ppermute | solution.py:299
  76.6 6.9 %collective-permute-start.37 = (bf16[512,256]{1,0:T(8,128)(2,1)S(1)}, bf16[512,256]{1,0:T(8,128)(2,1)S(1)}, u32[]{:S(2)}, u32[]{:S(2)}) collective-permute-start(bf16[512,256]{1,0:T(8,128)(2,1)S(1)} %get-tuple-element.196.refs_2_), channel_id=1, source_target_pairs={{0,1},{1,0},{4,5},{5,4},{8,9},{9,8},{12,13},{13,12},{14,15},{15,14... | collective-permute-start | bytes 786440 | tf_op jit(solution)/shard_map/ppermute | solution.py:300
  80.5 6.7 %collective-permute-start.35 = (bf16[512,256]{1,0:T(8,128)(2,1)S(1)}, bf16[512,256]{1,0:T(8,128)(2,1)S(1)}, u32[]{:S(2)}, u32[]{:S(2)}) collective-permute-start(bf16[512,256]{1,0:T(8,128)(2,1)S(1)} %collective-permute-done.34.refs_0_), channel_id=1, source_target_pairs={{0,4},{1,5},{4,8},{5,9},{8,12},{9,13},{12,14},{13,15},{14,10},{15,... | collective-permute-start | bytes 786440 | tf_op jit(solution)/shard_map/ppermute | solution.py:298
  83.0 6.9 %collective-permute-start.41 = (bf16[512,256]{1,0:T(8,128)(2,1)S(1)}, bf16[512,256]{1,0:T(8,128)(2,1)S(1)}, u32[]{:S(2)}, u32[]{:S(2)}) collective-permute-start(bf16[512,256]{1,0:T(8,128)(2,1)S(1)} %collective-permute-done.36.refs_1_), channel_id=1, source_target_pairs={{0,1},{1,0},{4,5},{5,4},{8,9},{9,8},{12,13},{13,12},{14,15},{15,14... | collective-permute-start | bytes 786440 | tf_op jit(solution)/shard_map/ppermute | solution.py:300
  89.3 7.3 %collective-permute-start.47 = (bf16[512,256]{1,0:T(8,128)(2,1)S(1)}, bf16[512,256]{1,0:T(8,128)(2,1)S(1)}, u32[]{:S(2)}, u32[]{:S(2)}) collective-permute-start(bf16[512,256]{1,0:T(8,128)(2,1)S(1)} %collective-permute-done.39.refs_1_), channel_id=1, source_target_pairs={{0,1},{1,0},{4,5},{5,4},{8,9},{9,8},{12,13},{13,12},{14,15},{15,14... | collective-permute-start | bytes 786440 | tf_op jit(solution)/shard_map/ppermute | solution.py:300
  89.4 9.0 %collective-permute-start.46 = (bf16[512,256]{1,0:T(8,128)(2,1)S(1)}, bf16[512,256]{1,0:T(8,128)(2,1)S(1)}, u32[]{:S(2)}, u32[]{:S(2)}) collective-permute-start(bf16[512,256]{1,0:T(8,128)(2,1)S(1)} %collective-permute-done.35.refs_0_), channel_id=1, source_target_pairs={{0,1},{1,0},{4,5},{5,4},{8,9},{9,8},{12,13},{13,12},{14,15},{15,14... | collective-permute-start | bytes 786440 | tf_op jit(solution)/shard_map/ppermute | solution.py:300
  107.7 6.5 %collective-permute-start.54 = (bf16[512,256]{1,0:T(8,128)(2,1)S(1)}, bf16[512,256]{1,0:T(8,128)(2,1)S(1)}, u32[]{:S(2)}, u32[]{:S(2)}) collective-permute-start(bf16[512,256]{1,0:T(8,128)(2,1)S(1)} %get-tuple-element.227), channel_id=1, source_target_pairs={{0,1},{1,0},{4,5},{5,4},{8,9},{9,8},{12,13},{13,12},{14,15},{15,14... | collective-permute-start | bytes 786440 | tf_op jit(solution)/shard_map/ppermute | solution.py:300
  107.9 6.9 %collective-permute-start.56 = (bf16[512,256]{1,0:T(8,128)(2,1)S(1)}, bf16[512,256]{1,0:T(8,128)(2,1)S(1)}, u32[]{:S(2)}, u32[]{:S(2)}) collective-permute-start(bf16[512,256]{1,0:T(8,128)(2,1)S(1)} %get-tuple-element.230), channel_id=1, source_target_pairs={{0,1},{1,0},{4,5},{5,4},{8,9},{9,8},{12,13},{13,12},{14,15},{15,14... | collective-permute-start | bytes 786440 | tf_op jit(solution)/shard_map/ppermute | solution.py:300
  114.3 8.1 %collective-permute-start.55 = (bf16[512,256]{1,0:T(8,128)(2,1)S(1)}, bf16[512,256]{1,0:T(8,128)(2,1)S(1)}, u32[]{:S(2)}, u32[]{:S(2)}) collective-permute-start(bf16[512,256]{1,0:T(8,128)(2,1)S(1)} %pad_maximum_fusion.2), channel_id=1, source_target_pairs={{0,4},{1,5},{4,8},{5,9},{8,12},{9,13},{12,14},{13,15},{14,10},{15,... | collective-permute-start | bytes 786440 | tf_op jit(solution)/shard_map/ppermute | solution.py:298
  115.0 7.7 %collective-permute-start.60 = (bf16[512,256]{1,0:T(8,128)(2,1)S(1)}, bf16[512,256]{1,0:T(8,128)(2,1)S(1)}, u32[]{:S(2)}, u32[]{:S(2)}) collective-permute-start(bf16[512,256]{1,0:T(8,128)(2,1)S(1)} %pad_maximum_fusion.3), channel_id=1, source_target_pairs={{4,0},{5,1},{8,4},{9,5},{12,8},{13,9},{14,12},{15,13},{10,14},{11,... | collective-permute-start | bytes 786440 | tf_op jit(solution)/shard_map/ppermute | solution.py:299
  116.6 6.6 %collective-permute-start.59 = (bf16[512,256]{1,0:T(8,128)(2,1)S(1)}, bf16[512,256]{1,0:T(8,128)(2,1)S(1)}, u32[]{:S(2)}, u32[]{:S(2)}) collective-permute-start(bf16[512,256]{1,0:T(8,128)(2,1)S(1)} %get-tuple-element.232), channel_id=1, source_target_pairs={{0,1},{1,0},{4,5},{5,4},{8,9},{9,8},{12,13},{13,12},{14,15},{15,14... | collective-permute-start | bytes 786440 | tf_op jit(solution)/shard_map/ppermute | solution.py:300
  122.8 6.9 %collective-permute-start.58 = (bf16[512,256]{1,0:T(8,128)(2,1)S(1)}, bf16[512,256]{1,0:T(8,128)(2,1)S(1)}, u32[]{:S(2)}, u32[]{:S(2)}) collective-permute-start(bf16[512,256]{1,0:T(8,128)(2,1)S(1)} %add_convert_fusion.4), channel_id=1, source_target_pairs={{0,4},{1,5},{4,8},{5,9},{8,12},{9,13},{12,14},{13,15},{14,10},{15,... | collective-permute-start | bytes 786440 | tf_op jit(solution)/shard_map/ppermute | solution.py:298
  123.3 6.5 %collective-permute-start.65 = (bf16[512,256]{1,0:T(8,128)(2,1)S(1)}, bf16[512,256]{1,0:T(8,128)(2,1)S(1)}, u32[]{:S(2)}, u32[]{:S(2)}) collective-permute-start(bf16[512,256]{1,0:T(8,128)(2,1)S(1)} %add_convert_fusion.3), channel_id=1, source_target_pairs={{4,0},{5,1},{8,4},{9,5},{12,8},{13,9},{14,12},{15,13},{10,14},{11,... | collective-permute-start | bytes 786440 | tf_op jit(solution)/shard_map/ppermute | solution.py:299
  132.1 9.7 %collective-permute-start.33 = (bf16[512,256]{1,0:T(8,128)(2,1)S(1)}, bf16[512,256]{1,0:T(8,128)(2,1)S(1)}, u32[]{:S(2)}, u32[]{:S(2)}) collective-permute-start(bf16[512,256]{1,0:T(8,128)(2,1)S(1)} %get-tuple-element.195), channel_id=1, source_target_pairs={{0,16},{1,17},{2,18},{3,19},{4,20},{5,21},{6,22},{7,23},{8,24},{9,... | collective-permute-start | bytes 786440 | tf_op jit(solution)/shard_map/ppermute | solution.py:420
  138.3 8.3 %collective-permute-start.67 = (bf16[512,256]{1,0:T(8,128)(2,1)S(1)}, bf16[512,256]{1,0:T(8,128)(2,1)S(1)}, u32[]{:S(2)}, u32[]{:S(2)}) collective-permute-start(bf16[512,256]{1,0:T(8,128)(2,1)S(1)} %add_convert_fusion), channel_id=1, source_target_pairs={{16,0},{17,1},{18,2},{19,3},{20,4},{21,5},{22,6},{23,7},{24,8},{25... | collective-permute-start | bytes 786440 | tf_op jit(solution)/shard_map/ppermute | solution.py:457
  (42 other events, 224.8 us)

commit v2 on v1

--- a/solution.py
+++ b/solution.py
@@ -150,8 +150,9 @@
 
 def turn_kernel(raw, out):
     tokens = raw.shape[2]
+    whole = raw[...].astype(f32)
     for t in range(raw.shape[1]):
-        out[t * tokens : (t + 1) * tokens, :] = raw[:, t, :].astype(f32).T.astype(out.dtype)
+        out[t * tokens : (t + 1) * tokens, :] = whole[:, t, :].T.astype(out.dtype)
 
 
 def turned(raw):
@@ -320,7 +321,10 @@
 
         for k in range(1, far + 1):
             sent = (fw[:half], bw[half:]) if k == far else (fw, bw)
-            next_fw, next_bw = send_fw(sent[0]), send_bw(sent[1])
+            if early:
+                next_fw, next_bw = send_fw(sent[0]), send_bw(sent[1])
+            else:
+                next_bw, next_fw = send_bw(sent[1]), send_fw(sent[0])
             if k == 1:
                 own = [(mine, (0, False))]
                 sib = own + swapped(own)
@@ -330,8 +334,10 @@
                 if k == far and early:
                     held, sib = taken(sib), []
             fw, bw = next_fw, next_bw
-            fw, held, _ = lax.optimization_barrier((fw, held, beside.get(k)))
-            bw = tied(bw, held)
+            bw, held, _ = lax.optimization_barrier((bw, held, beside.get(k)))
+            fw = tied(fw, (held, bw) if not early else held)
+            if early:
+                bw = tied(bw, held)
         own = [((fw, bw), (-far, False))]
         last = swapped(own)
         held = taken(own + sib)

time: 148 us -> 147 us (level)
    ppermute x16, waiting for transfers between devices: 28.6 us -> 17 us  [per_device(): send_fw = lambda v: lax.ppermute(v, 'dp', forward)]
    ppermute x16, waiting for transfers between devices: 13.6 us -> 24.6 us  [per_device(): send_bw = lambda v: lax.ppermute(v, 'dp', backward)]
    ppermute x16, starting transfers between devices: 24.3 us -> 17.5 us  [per_device(): send_fw = lambda v: lax.ppermute(v, 'dp', forward)]
    ppermute x16, starting transfers between devices: 11.3 us -> 17 us  [per_device(): send_bw = lambda v: lax.ppermute(v, 'dp', backward)]
    ppermute x1, waiting for transfers between devices: 2.12 us -> 3.65 us  [per_device(): lax.ppermute(emitted, 'section', [(s, s + 1) for s in range(sections - 1)])]
where the time goes in v2:
time: 147 us
  waiting for transfers between devices  49.1 us (33%)
  starting transfers between devices  47.1 us (32%)
  Pallas kernels  45.2 us (31%)
  local copies, waits for them, and re-layouts  2.85 us (2%)
    pallas_call x28, Pallas kernels, call(): pl.pallas_call(body, out_shape=[pltpu.VMEM(shape, dtype) for shape, dtype...  45.2 us
    ppermute x16, waiting for transfers between devices, per_device(): send_bw = lambda v: lax.ppermute(v, 'dp', backward)  24.6 us
    ppermute x16, starting transfers between devices, per_device(): send_fw = lambda v: lax.ppermute(v, 'dp', forward)  17.5 us
    ppermute x16, starting transfers between devices, per_device(): send_bw = lambda v: lax.ppermute(v, 'dp', backward)  17 us
    ppermute x16, waiting for transfers between devices, per_device(): send_fw = lambda v: lax.ppermute(v, 'dp', forward)  17 us
    ppermute x34, starting transfers between devices, per_device(): swap = lambda v: lax.ppermute(v, 'dp', sibling)  7.8 us
    ppermute x1, waiting for transfers between devices, per_device(): lax.ppermute(emitted, 'section', [(s, s + 1) for s in range(sections - 1)])  3.65 us
    ppermute x1, waiting for transfers between devices, per_device(): lax.ppermute(total.astype(bf16), 'section', [(s + 1, s) for s in range(se...  3.48 us
  transfers between devices with their start and end apart: 68, of which 28 were waited for; matrix products, arithmetic and copies ran while one was open for 1% of the time, Pallas kernels for 27%

profile of v2, /device:TPU:0, one launch (start us, length us, event | category | flops | bytes accessed | tf_op | source)
XLA Modules:
  0.0 146.8 jit_solution(18193368320691008175)
XLA Ops:
  2.0 3.0 %collective-permute-start.1 = (bf16[512,256]{1,0:T(8,128)(2,1)S(1)}, bf16[512,256]{1,0:T(8,128)(2,1)S(1)}, u32[]{:S(2)}, u32[]{:S(2)}) collective-permute-start(bf16[512,256]{1,0:T(8,128)(2,1)S(1)} %shard_map.104.refs_2_.refs_4_), channel_id=1, source_target_pairs={{4,0},{5,1},{8,4},{9,5},{12,8},{13,9},{14,12},{15,13},{10,14},{11,... | collective-permute-start | bytes 786440 | tf_op jit(solution)/shard_map/ppermute | solution.py:300
  5.2 5.8 %shard_map.105 = (bf16[4096,1024]{1,0:T(8,128)(2,1)S(1)}, bf16[4096,1024]{1,0:T(8,128)(2,1)S(1)}) custom-call(bf16[4096,1024]{1,0:T(8,128)(2,1)} %bitcast.16, bf16[4096,1024]{1,0:T(8,128)(2,1)} %bitcast.17), custom_call_target="tpu_custom_call" | custom-call | flops 1 | bytes 1 | tf_op jit(solution)/shard_map/pallas_call | solution.py:49
  11.4 1.7 %collective-permute-start.3 = (bf16[512,256]{1,0:T(8,128)(2,1)S(1)}, bf16[512,256]{1,0:T(8,128)(2,1)S(1)}, u32[]{:S(2)}, u32[]{:S(2)}) collective-permute-start(bf16[512,256]{1,0:T(8,128)(2,1)S(1)} %collective-permute-done.1.refs_1_), channel_id=1, source_target_pairs={{4,0},{5,1},{8,4},{9,5},{12,8},{13,9},{14,12},{15,13},{10,14},{11,... | collective-permute-start | bytes 786440 | tf_op jit(solution)/shard_map/ppermute | solution.py:300
  13.9 3.4 %shard_map.106 = (f32[512,1024]{1,0:T(8,128)S(1)}, f32[512,1024]{1,0:T(8,128)S(1)}, bf16[1024,4096]{1,0:T(8,128)(2,1)S(1)}) custom-call(bf16[512,256]{1,0:T(8,128)(2,1)S(1)} %collective-permute-done.refs_0_, bf16[512,256]{1,0:T(8,128)(2,1)S(1)} %collective-permute-done.1.refs_1_, bf16[512,256]{1,0:T(8,128)(2,1)S(1)} %shard_map.104.refs_2_.refs_4_, ...), custom_call_target="tpu_custom_call" | custom-call | flops 1 | bytes 1 | tf_op jit(solution)/shard_map/pallas_call | solution.py:49
  17.3 2.6 %collective-permute-done.3.refs_1_ = bf16[512,256]{1,0:T(8,128)(2,1)S(1)} collective-permute-done((bf16[512,256]{1,0:T(8,128)(2,1)S(1)}, bf16[512,256]{1,0:T(8,128)(2,1)S(1)}, u32[]{:S(2)}, u32[]{:S(2)}) %collective-permute-start.3) | collective-permute-done | bytes 262176 | tf_op jit(solution)/shard_map/ppermute | solution.py:300
  20.0 1.7 %collective-permute-start.6 = (bf16[512,256]{1,0:T(8,128)(2,1)S(1)}, bf16[512,256]{1,0:T(8,128)(2,1)S(1)}, u32[]{:S(2)}, u32[]{:S(2)}) collective-permute-start(bf16[512,256]{1,0:T(8,128)(2,1)S(1)} %collective-permute-done.3.refs_1_), channel_id=1, source_target_pairs={{4,0},{5,1},{8,4},{9,5},{12,8},{13,9},{14,12},{15,13},{10,14},{11,... | collective-permute-start | bytes 786440 | tf_op jit(solution)/shard_map/ppermute | solution.py:300
  22.5 2.7 %shard_map.107 = (f32[512,1024]{1,0:T(8,128)S(1)}, f32[512,1024]{1,0:T(8,128)S(1)}) custom-call(bf16[512,256]{1,0:T(8,128)(2,1)S(1)} %collective-permute-done.2.refs_0_, bf16[512,256]{1,0:T(8,128)(2,1)S(1)} %collective-permute-done.3.refs_1_, bf16[512,256]{1,0:T(8,128)(2,1)S(1)} %collective-permute-done.7.refs_2_, ...), custom_call_target="tpu_custom_call", output_to_operand_aliasing={{0}: (6, {}), {1}: (7, {})} | custom-call | flops 1 | bytes 1 | tf_op jit(solution)/shard_map/pallas_call | solution.py:49
  25.3 2.5 %collective-permute-done.6.refs_1_ = bf16[512,256]{1,0:T(8,128)(2,1)S(1)} collective-permute-done((bf16[512,256]{1,0:T(8,128)(2,1)S(1)}, bf16[512,256]{1,0:T(8,128)(2,1)S(1)}, u32[]{:S(2)}, u32[]{:S(2)}) %collective-permute-start.6) | collective-permute-done | bytes 262176 | tf_op jit(solution)/shard_map/ppermute | solution.py:300
  27.7 1.7 %collective-permute-start.10 = (bf16[256,256]{1,0:T(8,128)(2,1)S(1)}, bf16[256,256]{1,0:T(8,128)(2,1)S(1)}, u32[]{:S(2)}, u32[]{:S(2)}) collective-permute-start(bf16[256,256]{1,0:T(8,128)(2,1)S(1)} %slice.57), channel_id=1, source_target_pairs={{4,0},{5,1},{8,4},{9,5},{12,8},{13,9},{14,12},{15,13},{10,14},{11,... | collective-permute-start | bytes 393224 | tf_op jit(solution)/shard_map/ppermute | solution.py:300
  30.4 2.7 %shard_map.108 = (f32[512,1024]{1,0:T(8,128)S(1)}, f32[512,1024]{1,0:T(8,128)S(1)}) custom-call(bf16[512,256]{1,0:T(8,128)(2,1)S(1)} %collective-permute-done.5.refs_0_, bf16[512,256]{1,0:T(8,128)(2,1)S(1)} %collective-permute-done.6.refs_1_, bf16[512,256]{1,0:T(8,128)(2,1)S(1)} %collective-permute-done.11.refs_2_, ...), custom_call_target="tpu_custom_call", output_to_operand_aliasing={{0}: (6, {}), {1}: (7, {})} | custom-call | flops 1 | bytes 1 | tf_op jit(solution)/shard_map/pallas_call | solution.py:49
  35.0 2.2 %shard_map.109 = (f32[512,1024]{1,0:T(8,128)S(1)}, f32[512,1024]{1,0:T(8,128)S(1)}) custom-call(bf16[256,256]{1,0:T(8,128)(2,1)S(1)} %collective-permute-done.9.refs_0_, bf16[256,256]{1,0:T(8,128)(2,1)S(1)} %collective-permute-done.10.refs_1_, bf16[512,256]{1,0:T(8,128)(2,1)S(1)} %collective-permute-done.15.refs_2_, ...), custom_call_target="tpu_custom_call", output_to_operand_aliasing={{0}: (6, {}), {1}: (7, {})} | custom-call | flops 1 | bytes 1 | tf_op jit(solution)/shard_map/pallas_call | solution.py:49
  37.2 1.9 %shard_map.110 = (f32[512,1024]{1,0:T(8,128)S(1)}, f32[512,1024]{1,0:T(8,128)S(1)}, bf16[512,1024]{1,0:T(8,128)(2,1)S(1)}) custom-call(bf16[256,256]{1,0:T(8,128)(2,1)S(1)} %collective-permute-done.13.refs_0_, bf16[256,256]{1,0:T(8,128)(2,1)S(1)} %collective-permute-done.14.refs_1_, ...), custom_call_target="tpu_custom_call", output_to_operand_aliasing={{0}: (4, {}), {1}: (5, {})} | custom-call | flops 1 | bytes 1 | tf_op jit(solution)/shard_map/pallas_call | solution.py:49
  45.5 1.8 %collective-permute-done.18 = bf16[256,256]{1,0:T(8,128)(2,1)S(1)} collective-permute-done((bf16[256,256]{1,0:T(8,128)(2,1)S(1)}, bf16[256,256]{1,0:T(8,128)(2,1)S(1)}, u32[]{:S(2)}, u32[]{:S(2)}) %collective-permute-start.18) | collective-permute-done | bytes 131104 | tf_op jit(solution)/shard_map/ppermute | solution.py:299
  51.8 3.7 %collective-permute-done.21 = bf16[512,256]{1,0:T(8,128)(2,1)S(1)} collective-permute-done((bf16[512,256]{1,0:T(8,128)(2,1)S(1)}, bf16[512,256]{1,0:T(8,128)(2,1)S(1)}, u32[]{:S(2)}, u32[]{:S(2)}) %collective-permute-start.21) | collective-permute-done | bytes 262176 | tf_op jit(solution)/shard_map/ppermute | solution.py:299
  56.9 1.7 %collective-permute-start.24 = (bf16[512,256]{1,0:T(8,128)(2,1)S(1)}, bf16[512,256]{1,0:T(8,128)(2,1)S(1)}, u32[]{:S(2)}, u32[]{:S(2)}) collective-permute-start(bf16[512,256]{1,0:T(8,128)(2,1)S(1)} %add_convert_fusion.9), channel_id=1, source_target_pairs={{0,4},{1,5},{4,8},{5,9},{8,12},{9,13},{12,14},{13,15},{14,10},{15,... | collective-permute-start | bytes 786440 | tf_op jit(solution)/shard_map/ppermute | solution.py:299
  60.6 2.8 %collective-permute-done.24 = bf16[512,256]{1,0:T(8,128)(2,1)S(1)} collective-permute-done((bf16[512,256]{1,0:T(8,128)(2,1)S(1)}, bf16[512,256]{1,0:T(8,128)(2,1)S(1)}, u32[]{:S(2)}, u32[]{:S(2)}) %collective-permute-start.24) | collective-permute-done | bytes 262176 | tf_op jit(solution)/shard_map/ppermute | solution.py:299
  63.3 2.0 %collective-permute-done.31 = bf16[512,256]{1,0:T(8,128)(2,1)S(1)} collective-permute-done((bf16[512,256]{1,0:T(8,128)(2,1)S(1)}, bf16[512,256]{1,0:T(8,128)(2,1)S(1)}, u32[]{:S(2)}, u32[]{:S(2)}) %collective-permute-start.31) | collective-permute-done | bytes 262176 | tf_op jit(solution)/shard_map/ppermute | solution.py:300
  68.1 3.9 %collective-permute-done.32.refs_3_ = bf16[512,256]{1,0:T(8,128)(2,1)S(1)} collective-permute-done((bf16[512,256]{1,0:T(8,128)(2,1)S(1)}, bf16[512,256]{1,0:T(8,128)(2,1)S(1)}, u32[]{:S(2)}, u32[]{:S(2)}) %collective-permute-start.32) | collective-permute-done | bytes 262176 | tf_op jit(solution)/shard_map/ppermute | solution.py:300
  75.0 1.8 %shard_map.119 = (f32[512,1024]{1,0:T(8,128)S(1)}, f32[512,1024]{1,0:T(8,128)S(1)}, f32[512,1024]{1,0:T(8,128)S(1)}) custom-call(f32[512,1024]{1,0:T(8,128)S(1)} %get-tuple-element.203.refs_0_, f32[512,1024]{1,0:T(8,128)S(1)} %get-tuple-element.204.refs_1_, s32[1,1024]{1,0:T(1,128)S(1)} %copy-done.2, s32[1,1024]{1,0:T(1,128)S(1)} %copy-done.3), custom_call_target="tpu_custom_call" | custom-call | flops 268435456 | bytes 524288 | tf_op jit(solution)/shard_map/pallas_call | solution.py:49
  76.8 2.5 %collective-permute-done.36.refs_1_ = bf16[512,256]{1,0:T(8,128)(2,1)S(1)} collective-permute-done((bf16[512,256]{1,0:T(8,128)(2,1)S(1)}, bf16[512,256]{1,0:T(8,128)(2,1)S(1)}, u32[]{:S(2)}, u32[]{:S(2)}) %collective-permute-start.36) | collective-permute-done | bytes 262176 | tf_op jit(solution)/shard_map/ppermute | solution.py:300
  83.4 2.3 %collective-permute-done.37.refs_1_ = bf16[512,256]{1,0:T(8,128)(2,1)S(1)} collective-permute-done((bf16[512,256]{1,0:T(8,128)(2,1)S(1)}, bf16[512,256]{1,0:T(8,128)(2,1)S(1)}, u32[]{:S(2)}, u32[]{:S(2)}) %collective-permute-start.37) | collective-permute-done | bytes 262176 | tf_op jit(solution)/shard_map/ppermute | solution.py:300
  89.8 2.2 %collective-permute-done.40.refs_1_ = bf16[512,256]{1,0:T(8,128)(2,1)S(1)} collective-permute-done((bf16[512,256]{1,0:T(8,128)(2,1)S(1)}, bf16[512,256]{1,0:T(8,128)(2,1)S(1)}, u32[]{:S(2)}, u32[]{:S(2)}) %collective-permute-start.40) | collective-permute-done | bytes 262176 | tf_op jit(solution)/shard_map/ppermute | solution.py:300
  103.9 1.8 %shard_map.126 = (f32[512,256]{1,0:T(8,128)S(1)}, bf16[512,256]{1,0:T(8,128)(2,1)S(1)}, bf16[512,256]{1,0:T(8,128)(2,1)S(1)}) custom-call(bf16[512,1024]{1,0:T(8,128)(2,1)S(1)} %get-tuple-element.252.refs_0_, bf16[512,1024]{1,0:T(8,128)(2,1)S(1)} %get-tuple-element.219.refs_1_, bf16[4096,1024]{1,0:T(8,128)(2,1)S(1)} %get-tuple-element.134.refs_4_.refs_2_, ...), custom_call_target="tpu_custom_call" | custom-call | flops 1610612736 | bytes 3145728 | tf_op jit(solution)/shard_map/pallas_call | solution.py:49
  108.4 2.4 %shard_map.129 = (f32[512,256]{1,0:T(8,128)S(1)}, f32[512,256]{1,0:T(8,128)S(1)}, bf16[512,256]{1,0:T(8,128)(2,1)S(1)}, bf16[512,256]{1,0:T(8,128)(2,1)S(1)}) custom-call(bf16[512,1024]{1,0:T(8,128)(2,1)S(1)} %get-tuple-element.252.refs_0_, bf16[512,1024]{1,0:T(8,128)(2,1)S(1)} %get-tuple-element.219.refs_1_, ...), custom_call_target="tpu_custom_call" | custom-call | flops 2147483648 | bytes 4194304 | tf_op jit(solution)/shard_map/pallas_call | solution.py:49
  115.2 2.4 %shard_map.130 = (f32[512,256]{1,0:T(8,128)S(1)}, f32[512,256]{1,0:T(8,128)S(1)}, bf16[512,256]{1,0:T(8,128)(2,1)S(1)}, bf16[512,256]{1,0:T(8,128)(2,1)S(1)}) custom-call(bf16[512,1024]{1,0:T(8,128)(2,1)S(1)} %get-tuple-element.252.refs_0_, bf16[512,1024]{1,0:T(8,128)(2,1)S(1)} %get-tuple-element.219.refs_1_, ...), custom_call_target="tpu_custom_call" | custom-call | flops 2147483648 | bytes 4194304 | tf_op jit(solution)/shard_map/pallas_call | solution.py:49
  117.5 2.8 %collective-permute-done.55 = bf16[512,256]{1,0:T(8,128)(2,1)S(1)} collective-permute-done((bf16[512,256]{1,0:T(8,128)(2,1)S(1)}, bf16[512,256]{1,0:T(8,128)(2,1)S(1)}, u32[]{:S(2)}, u32[]{:S(2)}) %collective-permute-start.55) | collective-permute-done | bytes 262176 | tf_op jit(solution)/shard_map/ppermute | solution.py:299
  125.2 2.4 %collective-permute-done.58 = bf16[512,256]{1,0:T(8,128)(2,1)S(1)} collective-permute-done((bf16[512,256]{1,0:T(8,128)(2,1)S(1)}, bf16[512,256]{1,0:T(8,128)(2,1)S(1)}, u32[]{:S(2)}, u32[]{:S(2)}) %collective-permute-start.58) | collective-permute-done | bytes 262176 | tf_op jit(solution)/shard_map/ppermute | solution.py:299
  127.6 2.1 %collective-permute-done.65 = bf16[512,256]{1,0:T(8,128)(2,1)S(1)} collective-permute-done((bf16[512,256]{1,0:T(8,128)(2,1)S(1)}, bf16[512,256]{1,0:T(8,128)(2,1)S(1)}, u32[]{:S(2)}, u32[]{:S(2)}) %collective-permute-start.65) | collective-permute-done | bytes 262176 | tf_op jit(solution)/shard_map/ppermute | solution.py:300
  130.1 1.9 %collective-permute-start.63 = (bf16[512,256]{1,0:T(8,128)(2,1)S(1)}, bf16[512,256]{1,0:T(8,128)(2,1)S(1)}, u32[]{:S(2)}, u32[]{:S(2)}) collective-permute-start(bf16[512,256]{1,0:T(8,128)(2,1)S(1)} %add_convert_fusion.2), channel_id=1, source_target_pairs={{0,4},{1,5},{4,8},{5,9},{8,12},{9,13},{12,14},{13,15},{14,10},{15,... | collective-permute-start | bytes 786440 | tf_op jit(solution)/shard_map/ppermute | solution.py:299
  132.0 3.4 %collective-permute-start.33 = (bf16[512,256]{1,0:T(8,128)(2,1)S(1)}, bf16[512,256]{1,0:T(8,128)(2,1)S(1)}, u32[]{:S(2)}, u32[]{:S(2)}) collective-permute-start(bf16[512,256]{1,0:T(8,128)(2,1)S(1)} %get-tuple-element.200), channel_id=1, source_target_pairs={{0,16},{1,17},{2,18},{3,19},{4,20},{5,21},{6,22},{7,23},{8,24},{9,... | collective-permute-start | bytes 786440 | tf_op jit(solution)/shard_map/ppermute | solution.py:426
  137.9 3.7 %collective-permute-done.33 = bf16[512,256]{1,0:T(8,128)(2,1)S(1)} collective-permute-done((bf16[512,256]{1,0:T(8,128)(2,1)S(1)}, bf16[512,256]{1,0:T(8,128)(2,1)S(1)}, u32[]{:S(2)}, u32[]{:S(2)}) %collective-permute-start.33) | collective-permute-done | bytes 262176 | tf_op jit(solution)/shard_map/ppermute | solution.py:426
  142.5 3.5 %collective-permute-done.67 = bf16[512,256]{1,0:T(8,128)(2,1)S(1)} collective-permute-done((bf16[512,256]{1,0:T(8,128)(2,1)S(1)}, bf16[512,256]{1,0:T(8,128)(2,1)S(1)}, u32[]{:S(2)}, u32[]{:S(2)}) %collective-permute-start.67) | collective-permute-done | bytes 262176 | tf_op jit(solution)/shard_map/ppermute | solution.py:463
  (178 shorter events, 62.9 us)
Async XLA Ops:
  2.0 9.4 %collective-permute-start.1 = (bf16[512,256]{1,0:T(8,128)(2,1)S(1)}, bf16[512,256]{1,0:T(8,128)(2,1)S(1)}, u32[]{:S(2)}, u32[]{:S(2)}) collective-permute-start(bf16[512,256]{1,0:T(8,128)(2,1)S(1)} %shard_map.104.refs_2_.refs_4_), channel_id=1, source_target_pairs={{4,0},{5,1},{8,4},{9,5},{12,8},{13,9},{14,12},{15,13},{10,14},{11,... | collective-permute-start | bytes 786440 | tf_op jit(solution)/shard_map/ppermute | solution.py:300
  5.0 8.0 %collective-permute-start = (bf16[512,256]{1,0:T(8,128)(2,1)S(1)}, bf16[512,256]{1,0:T(8,128)(2,1)S(1)}, u32[]{:S(2)}, u32[]{:S(2)}) collective-permute-start(bf16[512,256]{1,0:T(8,128)(2,1)S(1)} %shard_map.104.refs_2_.refs_4_), channel_id=1, source_target_pairs={{0,4},{1,5},{4,8},{5,9},{8,12},{9,13},{12,14},{13,15},{14,10},{15,... | collective-permute-start | bytes 786440 | tf_op jit(solution)/shard_map/ppermute | solution.py:299
  5.2 8.8 %collective-permute-start.4 = (bf16[512,256]{1,0:T(8,128)(2,1)S(1)}, bf16[512,256]{1,0:T(8,128)(2,1)S(1)}, u32[]{:S(2)}, u32[]{:S(2)}) collective-permute-start(bf16[512,256]{1,0:T(8,128)(2,1)S(1)} %shard_map.104.refs_2_.refs_4_), channel_id=1, source_target_pairs={{0,1},{1,0},{4,5},{5,4},{8,9},{9,8},{12,13},{13,12},{14,15},{15,14... | collective-permute-start | bytes 786440 | tf_op jit(solution)/shard_map/ppermute | solution.py:301
  11.4 8.6 %collective-permute-start.3 = (bf16[512,256]{1,0:T(8,128)(2,1)S(1)}, bf16[512,256]{1,0:T(8,128)(2,1)S(1)}, u32[]{:S(2)}, u32[]{:S(2)}) collective-permute-start(bf16[512,256]{1,0:T(8,128)(2,1)S(1)} %collective-permute-done.1.refs_1_), channel_id=1, source_target_pairs={{4,0},{5,1},{8,4},{9,5},{12,8},{13,9},{14,12},{15,13},{10,14},{11,... | collective-permute-start | bytes 786440 | tf_op jit(solution)/shard_map/ppermute | solution.py:300
  13.1 8.6 %collective-permute-start.2 = (bf16[512,256]{1,0:T(8,128)(2,1)S(1)}, bf16[512,256]{1,0:T(8,128)(2,1)S(1)}, u32[]{:S(2)}, u32[]{:S(2)}) collective-permute-start(bf16[512,256]{1,0:T(8,128)(2,1)S(1)} %collective-permute-done.refs_0_), channel_id=1, source_target_pairs={{0,4},{1,5},{4,8},{5,9},{8,12},{9,13},{12,14},{13,15},{14,10},{15,... | collective-permute-start | bytes 786440 | tf_op jit(solution)/shard_map/ppermute | solution.py:299
  13.4 8.6 %collective-permute-start.7 = (bf16[512,256]{1,0:T(8,128)(2,1)S(1)}, bf16[512,256]{1,0:T(8,128)(2,1)S(1)}, u32[]{:S(2)}, u32[]{:S(2)}) collective-permute-start(bf16[512,256]{1,0:T(8,128)(2,1)S(1)} %collective-permute-done.refs_0_), channel_id=1, source_target_pairs={{0,1},{1,0},{4,5},{5,4},{8,9},{9,8},{12,13},{13,12},{14,15},{15,14... | collective-permute-start | bytes 786440 | tf_op jit(solution)/shard_map/ppermute | solution.py:301
  13.4 9.1 %collective-permute-start.8 = (bf16[512,256]{1,0:T(8,128)(2,1)S(1)}, bf16[512,256]{1,0:T(8,128)(2,1)S(1)}, u32[]{:S(2)}, u32[]{:S(2)}) collective-permute-start(bf16[512,256]{1,0:T(8,128)(2,1)S(1)} %collective-permute-done.1.refs_1_), channel_id=1, source_target_pairs={{0,1},{1,0},{4,5},{5,4},{8,9},{9,8},{12,13},{13,12},{14,15},{15,14... | collective-permute-start | bytes 786440 | tf_op jit(solution)/shard_map/ppermute | solution.py:301
  20.0 7.8 %collective-permute-start.6 = (bf16[512,256]{1,0:T(8,128)(2,1)S(1)}, bf16[512,256]{1,0:T(8,128)(2,1)S(1)}, u32[]{:S(2)}, u32[]{:S(2)}) collective-permute-start(bf16[512,256]{1,0:T(8,128)(2,1)S(1)} %collective-permute-done.3.refs_1_), channel_id=1, source_target_pairs={{4,0},{5,1},{8,4},{9,5},{12,8},{13,9},{14,12},{15,13},{10,14},{11,... | collective-permute-start | bytes 786440 | tf_op jit(solution)/shard_map/ppermute | solution.py:300
  21.6 7.8 %collective-permute-start.5 = (bf16[512,256]{1,0:T(8,128)(2,1)S(1)}, bf16[512,256]{1,0:T(8,128)(2,1)S(1)}, u32[]{:S(2)}, u32[]{:S(2)}) collective-permute-start(bf16[512,256]{1,0:T(8,128)(2,1)S(1)} %collective-permute-done.2.refs_0_), channel_id=1, source_target_pairs={{0,4},{1,5},{4,8},{5,9},{8,12},{9,13},{12,14},{13,15},{14,10},{15,... | collective-permute-start | bytes 786440 | tf_op jit(solution)/shard_map/ppermute | solution.py:299
  22.0 7.9 %collective-permute-start.11 = (bf16[512,256]{1,0:T(8,128)(2,1)S(1)}, bf16[512,256]{1,0:T(8,128)(2,1)S(1)}, u32[]{:S(2)}, u32[]{:S(2)}) collective-permute-start(bf16[512,256]{1,0:T(8,128)(2,1)S(1)} %collective-permute-done.2.refs_0_), channel_id=1, source_target_pairs={{0,1},{1,0},{4,5},{5,4},{8,9},{9,8},{12,13},{13,12},{14,15},{15,14... | collective-permute-start | bytes 786440 | tf_op jit(solution)/shard_map/ppermute | solution.py:301
  22.0 8.4 %collective-permute-start.12 = (bf16[512,256]{1,0:T(8,128)(2,1)S(1)}, bf16[512,256]{1,0:T(8,128)(2,1)S(1)}, u32[]{:S(2)}, u32[]{:S(2)}) collective-permute-start(bf16[512,256]{1,0:T(8,128)(2,1)S(1)} %collective-permute-done.3.refs_1_), channel_id=1, source_target_pairs={{0,1},{1,0},{4,5},{5,4},{8,9},{9,8},{12,13},{13,12},{14,15},{15,14... | collective-permute-start | bytes 786440 | tf_op jit(solution)/shard_map/ppermute | solution.py:301
  40.8 6.8 %collective-permute-start.20 = (bf16[512,256]{1,0:T(8,128)(2,1)S(1)}, bf16[512,256]{1,0:T(8,128)(2,1)S(1)}, u32[]{:S(2)}, u32[]{:S(2)}) collective-permute-start(bf16[512,256]{1,0:T(8,128)(2,1)S(1)} %get-tuple-element.172), channel_id=1, source_target_pairs={{0,1},{1,0},{4,5},{5,4},{8,9},{9,8},{12,13},{13,12},{14,15},{15,14... | collective-permute-start | bytes 786440 | tf_op jit(solution)/shard_map/ppermute | solution.py:301
  47.8 7.7 %collective-permute-start.21 = (bf16[512,256]{1,0:T(8,128)(2,1)S(1)}, bf16[512,256]{1,0:T(8,128)(2,1)S(1)}, u32[]{:S(2)}, u32[]{:S(2)}) collective-permute-start(bf16[512,256]{1,0:T(8,128)(2,1)S(1)} %pad_maximum_fusion), channel_id=1, source_target_pairs={{0,4},{1,5},{4,8},{5,9},{8,12},{9,13},{12,14},{13,15},{14,10},{15,... | collective-permute-start | bytes 786440 | tf_op jit(solution)/shard_map/ppermute | solution.py:299
  49.5 7.3 %collective-permute-start.26 = (bf16[512,256]{1,0:T(8,128)(2,1)S(1)}, bf16[512,256]{1,0:T(8,128)(2,1)S(1)}, u32[]{:S(2)}, u32[]{:S(2)}) collective-permute-start(bf16[512,256]{1,0:T(8,128)(2,1)S(1)} %pad_maximum_fusion.1), channel_id=1, source_target_pairs={{4,0},{5,1},{8,4},{9,5},{12,8},{13,9},{14,12},{15,13},{10,14},{11,... | collective-permute-start | bytes 786440 | tf_op jit(solution)/shard_map/ppermute | solution.py:300
  50.0 6.8 %collective-permute-start.19 = (bf16[512,256]{1,0:T(8,128)(2,1)S(1)}, bf16[512,256]{1,0:T(8,128)(2,1)S(1)}, u32[]{:S(2)}, u32[]{:S(2)}) collective-permute-start(bf16[512,256]{1,0:T(8,128)(2,1)S(1)} %get-tuple-element.170), channel_id=1, source_target_pairs={{0,1},{1,0},{4,5},{5,4},{8,9},{9,8},{12,13},{13,12},{14,15},{15,14... | collective-permute-start | bytes 786440 | tf_op jit(solution)/shard_map/ppermute | solution.py:301
  50.0 8.5 %collective-permute-start.25 = (bf16[512,256]{1,0:T(8,128)(2,1)S(1)}, bf16[512,256]{1,0:T(8,128)(2,1)S(1)}, u32[]{:S(2)}, u32[]{:S(2)}) collective-permute-start(bf16[512,256]{1,0:T(8,128)(2,1)S(1)} %get-tuple-element.177), channel_id=1, source_target_pairs={{0,1},{1,0},{4,5},{5,4},{8,9},{9,8},{12,13},{13,12},{14,15},{15,14... | collective-permute-start | bytes 786440 | tf_op jit(solution)/shard_map/ppermute | solution.py:301
  56.9 6.4 %collective-permute-start.24 = (bf16[512,256]{1,0:T(8,128)(2,1)S(1)}, bf16[512,256]{1,0:T(8,128)(2,1)S(1)}, u32[]{:S(2)}, u32[]{:S(2)}) collective-permute-start(bf16[512,256]{1,0:T(8,128)(2,1)S(1)} %add_convert_fusion.9), channel_id=1, source_target_pairs={{0,4},{1,5},{4,8},{5,9},{8,12},{9,13},{12,14},{13,15},{14,10},{15,... | collective-permute-start | bytes 786440 | tf_op jit(solution)/shard_map/ppermute | solution.py:299
  58.7 6.7 %collective-permute-start.31 = (bf16[512,256]{1,0:T(8,128)(2,1)S(1)}, bf16[512,256]{1,0:T(8,128)(2,1)S(1)}, u32[]{:S(2)}, u32[]{:S(2)}) collective-permute-start(bf16[512,256]{1,0:T(8,128)(2,1)S(1)} %add_convert_fusion.8), channel_id=1, source_target_pairs={{4,0},{5,1},{8,4},{9,5},{12,8},{13,9},{14,12},{15,13},{10,14},{11,... | collective-permute-start | bytes 786440 | tf_op jit(solution)/shard_map/ppermute | solution.py:300
  65.6 6.4 %collective-permute-start.32 = (bf16[512,256]{1,0:T(8,128)(2,1)S(1)}, bf16[512,256]{1,0:T(8,128)(2,1)S(1)}, u32[]{:S(2)}, u32[]{:S(2)}) collective-permute-start(bf16[512,256]{1,0:T(8,128)(2,1)S(1)} %add_convert_fusion.6), channel_id=1, source_target_pairs={{4,0},{5,1},{8,4},{9,5},{12,8},{13,9},{14,12},{15,13},{10,14},{11,... | collective-permute-start | bytes 786440 | tf_op jit(solution)/shard_map/ppermute | solution.py:300
  75.0 6.9 %collective-permute-start.38 = (bf16[512,256]{1,0:T(8,128)(2,1)S(1)}, bf16[512,256]{1,0:T(8,128)(2,1)S(1)}, u32[]{:S(2)}, u32[]{:S(2)}) collective-permute-start(bf16[512,256]{1,0:T(8,128)(2,1)S(1)} %get-tuple-element.201.refs_2_), channel_id=1, source_target_pairs={{0,1},{1,0},{4,5},{5,4},{8,9},{9,8},{12,13},{13,12},{14,15},{15,14... | collective-permute-start | bytes 786440 | tf_op jit(solution)/shard_map/ppermute | solution.py:301
  81.4 6.9 %collective-permute-start.41 = (bf16[512,256]{1,0:T(8,128)(2,1)S(1)}, bf16[512,256]{1,0:T(8,128)(2,1)S(1)}, u32[]{:S(2)}, u32[]{:S(2)}) collective-permute-start(bf16[512,256]{1,0:T(8,128)(2,1)S(1)} %collective-permute-done.34.refs_0_), channel_id=1, source_target_pairs={{0,1},{1,0},{4,5},{5,4},{8,9},{9,8},{12,13},{13,12},{14,15},{15,14... | collective-permute-start | bytes 786440 | tf_op jit(solution)/shard_map/ppermute | solution.py:301
  87.7 7.0 %collective-permute-start.47 = (bf16[512,256]{1,0:T(8,128)(2,1)S(1)}, bf16[512,256]{1,0:T(8,128)(2,1)S(1)}, u32[]{:S(2)}, u32[]{:S(2)}) collective-permute-start(bf16[512,256]{1,0:T(8,128)(2,1)S(1)} %collective-permute-done.35.refs_0_), channel_id=1, source_target_pairs={{0,1},{1,0},{4,5},{5,4},{8,9},{9,8},{12,13},{13,12},{14,15},{15,14... | collective-permute-start | bytes 786440 | tf_op jit(solution)/shard_map/ppermute | solution.py:301
  87.7 7.4 %collective-permute-start.48 = (bf16[512,256]{1,0:T(8,128)(2,1)S(1)}, bf16[512,256]{1,0:T(8,128)(2,1)S(1)}, u32[]{:S(2)}, u32[]{:S(2)}) collective-permute-start(bf16[512,256]{1,0:T(8,128)(2,1)S(1)} %collective-permute-done.37.refs_1_), channel_id=1, source_target_pairs={{0,1},{1,0},{4,5},{5,4},{8,9},{9,8},{12,13},{13,12},{14,15},{15,14... | collective-permute-start | bytes 786440 | tf_op jit(solution)/shard_map/ppermute | solution.py:301
  105.7 6.5 %collective-permute-start.54 = (bf16[512,256]{1,0:T(8,128)(2,1)S(1)}, bf16[512,256]{1,0:T(8,128)(2,1)S(1)}, u32[]{:S(2)}, u32[]{:S(2)}) collective-permute-start(bf16[512,256]{1,0:T(8,128)(2,1)S(1)} %get-tuple-element.232), channel_id=1, source_target_pairs={{0,1},{1,0},{4,5},{5,4},{8,9},{9,8},{12,13},{13,12},{14,15},{15,14... | collective-permute-start | bytes 786440 | tf_op jit(solution)/shard_map/ppermute | solution.py:301
  105.9 7.9 %collective-permute-start.56 = (bf16[512,256]{1,0:T(8,128)(2,1)S(1)}, bf16[512,256]{1,0:T(8,128)(2,1)S(1)}, u32[]{:S(2)}, u32[]{:S(2)}) collective-permute-start(bf16[512,256]{1,0:T(8,128)(2,1)S(1)} %get-tuple-element.235), channel_id=1, source_target_pairs={{0,1},{1,0},{4,5},{5,4},{8,9},{9,8},{12,13},{13,12},{14,15},{15,14... | collective-permute-start | bytes 786440 | tf_op jit(solution)/shard_map/ppermute | solution.py:301
  112.3 8.0 %collective-permute-start.55 = (bf16[512,256]{1,0:T(8,128)(2,1)S(1)}, bf16[512,256]{1,0:T(8,128)(2,1)S(1)}, u32[]{:S(2)}, u32[]{:S(2)}) collective-permute-start(bf16[512,256]{1,0:T(8,128)(2,1)S(1)} %pad_maximum_fusion.2), channel_id=1, source_target_pairs={{0,4},{1,5},{4,8},{5,9},{8,12},{9,13},{12,14},{13,15},{14,10},{15,... | collective-permute-start | bytes 786440 | tf_op jit(solution)/shard_map/ppermute | solution.py:299
  114.0 7.0 %collective-permute-start.60 = (bf16[512,256]{1,0:T(8,128)(2,1)S(1)}, bf16[512,256]{1,0:T(8,128)(2,1)S(1)}, u32[]{:S(2)}, u32[]{:S(2)}) collective-permute-start(bf16[512,256]{1,0:T(8,128)(2,1)S(1)} %pad_maximum_fusion.3), channel_id=1, source_target_pairs={{4,0},{5,1},{8,4},{9,5},{12,8},{13,9},{14,12},{15,13},{10,14},{11,... | collective-permute-start | bytes 786440 | tf_op jit(solution)/shard_map/ppermute | solution.py:300
  114.6 8.1 %collective-permute-start.59 = (bf16[512,256]{1,0:T(8,128)(2,1)S(1)}, bf16[512,256]{1,0:T(8,128)(2,1)S(1)}, u32[]{:S(2)}, u32[]{:S(2)}) collective-permute-start(bf16[512,256]{1,0:T(8,128)(2,1)S(1)} %get-tuple-element.237), channel_id=1, source_target_pairs={{0,1},{1,0},{4,5},{5,4},{8,9},{9,8},{12,13},{13,12},{14,15},{15,14... | collective-permute-start | bytes 786440 | tf_op jit(solution)/shard_map/ppermute | solution.py:301
  122.9 6.8 %collective-permute-start.65 = (bf16[512,256]{1,0:T(8,128)(2,1)S(1)}, bf16[512,256]{1,0:T(8,128)(2,1)S(1)}, u32[]{:S(2)}, u32[]{:S(2)}) collective-permute-start(bf16[512,256]{1,0:T(8,128)(2,1)S(1)} %add_convert_fusion.3), channel_id=1, source_target_pairs={{4,0},{5,1},{8,4},{9,5},{12,8},{13,9},{14,12},{15,13},{10,14},{11,... | collective-permute-start | bytes 786440 | tf_op jit(solution)/shard_map/ppermute | solution.py:300
  129.9 6.4 %collective-permute-start.66 = (bf16[512,256]{1,0:T(8,128)(2,1)S(1)}, bf16[512,256]{1,0:T(8,128)(2,1)S(1)}, u32[]{:S(2)}, u32[]{:S(2)}) collective-permute-start(bf16[512,256]{1,0:T(8,128)(2,1)S(1)} %add_convert_fusion.1), channel_id=1, source_target_pairs={{4,0},{5,1},{8,4},{9,5},{12,8},{13,9},{14,12},{15,13},{10,14},{11,... | collective-permute-start | bytes 786440 | tf_op jit(solution)/shard_map/ppermute | solution.py:300
  132.0 9.6 %collective-permute-start.33 = (bf16[512,256]{1,0:T(8,128)(2,1)S(1)}, bf16[512,256]{1,0:T(8,128)(2,1)S(1)}, u32[]{:S(2)}, u32[]{:S(2)}) collective-permute-start(bf16[512,256]{1,0:T(8,128)(2,1)S(1)} %get-tuple-element.200), channel_id=1, source_target_pairs={{0,16},{1,17},{2,18},{3,19},{4,20},{5,21},{6,22},{7,23},{8,24},{9,... | collective-permute-start | bytes 786440 | tf_op jit(solution)/shard_map/ppermute | solution.py:426
  136.6 9.3 %collective-permute-start.67 = (bf16[512,256]{1,0:T(8,128)(2,1)S(1)}, bf16[512,256]{1,0:T(8,128)(2,1)S(1)}, u32[]{:S(2)}, u32[]{:S(2)}) collective-permute-start(bf16[512,256]{1,0:T(8,128)(2,1)S(1)} %add_convert_fusion), channel_id=1, source_target_pairs={{16,0},{17,1},{18,2},{19,3},{20,4},{21,5},{22,6},{23,7},{24,8},{25... | collective-permute-start | bytes 786440 | tf_op jit(solution)/shard_map/ppermute | solution.py:463
  (42 other events, 225.9 us)

commit v3 on v2

--- a/solution.py
+++ b/solution.py
@@ -239,7 +239,7 @@
         refs[0][:, hid] = (grad * to_gate[:, hid]).astype(bf16)
         refs[1][:, hid] = (grad * to_up[:, hid]).astype(bf16)
 
-    over_tiles(down.shape[0], 512, work)
+    over_tiles(down.shape[0], 512 if last else 1024, work)
 
 
 def slopes_kernel(steps, tokens, gate, up, threshold_ref, width_ref, slope, to_gate, to_up):

time: 147 us -> 147 us (level)
  transfers between devices with their start and end apart: 68 -> 68, of which waited for: 28 -> 29; matrix products, arithmetic and copies ran while one was open for 1% -> 1% of each run, Pallas kernels for 27% -> 26%
where the time goes in v3:
time: 147 us
  waiting for transfers between devices  50.2 us (34%)
  starting transfers between devices  47.1 us (32%)
  Pallas kernels  44.2 us (30%)
  local copies, waits for them, and re-layouts  2.85 us (2%)
    pallas_call x28, Pallas kernels, call(): pl.pallas_call(body, out_shape=[pltpu.VMEM(shape, dtype) for shape, dtype...  44.2 us
    ppermute x16, waiting for transfers between devices, per_device(): send_bw = lambda v: lax.ppermute(v, 'dp', backward)  25.3 us
    ppermute x16, starting transfers between devices, per_device(): send_fw = lambda v: lax.ppermute(v, 'dp', forward)  17.5 us
    ppermute x16, waiting for transfers between devices, per_device(): send_fw = lambda v: lax.ppermute(v, 'dp', forward)  17.2 us
    ppermute x16, starting transfers between devices, per_device(): send_bw = lambda v: lax.ppermute(v, 'dp', backward)  17 us
    ppermute x34, starting transfers between devices, per_device(): swap = lambda v: lax.ppermute(v, 'dp', sibling)  7.8 us
    ppermute x1, waiting for transfers between devices, per_device(): lax.ppermute(emitted, 'section', [(s, s + 1) for s in range(sections - 1)])  3.67 us
    ppermute x1, waiting for transfers between devices, per_device(): lax.ppermute(total.astype(bf16), 'section', [(s + 1, s) for s in range(se...  3.48 us
  transfers between devices with their start and end apart: 68, of which 29 were waited for; matrix products, arithmetic and copies ran while one was open for 1% of the time, Pallas kernels for 26%

profile of v3, /device:TPU:0, one launch (start us, length us, event | category | flops | bytes accessed | tf_op | source)
XLA Modules:
  0.0 146.9 jit_solution(6840869286108603268)
XLA Ops:
  2.0 3.0 %collective-permute-start.1 = (bf16[512,256]{1,0:T(8,128)(2,1)S(1)}, bf16[512,256]{1,0:T(8,128)(2,1)S(1)}, u32[]{:S(2)}, u32[]{:S(2)}) collective-permute-start(bf16[512,256]{1,0:T(8,128)(2,1)S(1)} %shard_map.104.refs_2_.refs_4_), channel_id=1, source_target_pairs={{4,0},{5,1},{8,4},{9,5},{12,8},{13,9},{14,12},{15,13},{10,14},{11,... | collective-permute-start | bytes 786440 | tf_op jit(solution)/shard_map/ppermute | solution.py:300
  5.2 5.8 %shard_map.105 = (bf16[4096,1024]{1,0:T(8,128)(2,1)S(1)}, bf16[4096,1024]{1,0:T(8,128)(2,1)S(1)}) custom-call(bf16[4096,1024]{1,0:T(8,128)(2,1)} %bitcast.16, bf16[4096,1024]{1,0:T(8,128)(2,1)} %bitcast.17), custom_call_target="tpu_custom_call" | custom-call | flops 1 | bytes 1 | tf_op jit(solution)/shard_map/pallas_call | solution.py:49
  11.4 1.7 %collective-permute-start.3 = (bf16[512,256]{1,0:T(8,128)(2,1)S(1)}, bf16[512,256]{1,0:T(8,128)(2,1)S(1)}, u32[]{:S(2)}, u32[]{:S(2)}) collective-permute-start(bf16[512,256]{1,0:T(8,128)(2,1)S(1)} %collective-permute-done.1.refs_1_), channel_id=1, source_target_pairs={{4,0},{5,1},{8,4},{9,5},{12,8},{13,9},{14,12},{15,13},{10,14},{11,... | collective-permute-start | bytes 786440 | tf_op jit(solution)/shard_map/ppermute | solution.py:300
  13.9 3.4 %shard_map.106 = (f32[512,1024]{1,0:T(8,128)S(1)}, f32[512,1024]{1,0:T(8,128)S(1)}, bf16[1024,4096]{1,0:T(8,128)(2,1)S(1)}) custom-call(bf16[512,256]{1,0:T(8,128)(2,1)S(1)} %collective-permute-done.refs_0_, bf16[512,256]{1,0:T(8,128)(2,1)S(1)} %collective-permute-done.1.refs_1_, bf16[512,256]{1,0:T(8,128)(2,1)S(1)} %shard_map.104.refs_2_.refs_4_, ...), custom_call_target="tpu_custom_call" | custom-call | flops 1 | bytes 1 | tf_op jit(solution)/shard_map/pallas_call | solution.py:49
  17.3 2.6 %collective-permute-done.3.refs_1_ = bf16[512,256]{1,0:T(8,128)(2,1)S(1)} collective-permute-done((bf16[512,256]{1,0:T(8,128)(2,1)S(1)}, bf16[512,256]{1,0:T(8,128)(2,1)S(1)}, u32[]{:S(2)}, u32[]{:S(2)}) %collective-permute-start.3) | collective-permute-done | bytes 262176 | tf_op jit(solution)/shard_map/ppermute | solution.py:300
  20.0 1.7 %collective-permute-start.6 = (bf16[512,256]{1,0:T(8,128)(2,1)S(1)}, bf16[512,256]{1,0:T(8,128)(2,1)S(1)}, u32[]{:S(2)}, u32[]{:S(2)}) collective-permute-start(bf16[512,256]{1,0:T(8,128)(2,1)S(1)} %collective-permute-done.3.refs_1_), channel_id=1, source_target_pairs={{4,0},{5,1},{8,4},{9,5},{12,8},{13,9},{14,12},{15,13},{10,14},{11,... | collective-permute-start | bytes 786440 | tf_op jit(solution)/shard_map/ppermute | solution.py:300
  22.5 2.7 %shard_map.107 = (f32[512,1024]{1,0:T(8,128)S(1)}, f32[512,1024]{1,0:T(8,128)S(1)}) custom-call(bf16[512,256]{1,0:T(8,128)(2,1)S(1)} %collective-permute-done.2.refs_0_, bf16[512,256]{1,0:T(8,128)(2,1)S(1)} %collective-permute-done.3.refs_1_, bf16[512,256]{1,0:T(8,128)(2,1)S(1)} %collective-permute-done.7.refs_2_, ...), custom_call_target="tpu_custom_call", output_to_operand_aliasing={{0}: (6, {}), {1}: (7, {})} | custom-call | flops 1 | bytes 1 | tf_op jit(solution)/shard_map/pallas_call | solution.py:49
  25.3 2.5 %collective-permute-done.6.refs_1_ = bf16[512,256]{1,0:T(8,128)(2,1)S(1)} collective-permute-done((bf16[512,256]{1,0:T(8,128)(2,1)S(1)}, bf16[512,256]{1,0:T(8,128)(2,1)S(1)}, u32[]{:S(2)}, u32[]{:S(2)}) %collective-permute-start.6) | collective-permute-done | bytes 262176 | tf_op jit(solution)/shard_map/ppermute | solution.py:300
  27.7 1.7 %collective-permute-start.10 = (bf16[256,256]{1,0:T(8,128)(2,1)S(1)}, bf16[256,256]{1,0:T(8,128)(2,1)S(1)}, u32[]{:S(2)}, u32[]{:S(2)}) collective-permute-start(bf16[256,256]{1,0:T(8,128)(2,1)S(1)} %slice.57), channel_id=1, source_target_pairs={{4,0},{5,1},{8,4},{9,5},{12,8},{13,9},{14,12},{15,13},{10,14},{11,... | collective-permute-start | bytes 393224 | tf_op jit(solution)/shard_map/ppermute | solution.py:300
  30.4 2.7 %shard_map.108 = (f32[512,1024]{1,0:T(8,128)S(1)}, f32[512,1024]{1,0:T(8,128)S(1)}) custom-call(bf16[512,256]{1,0:T(8,128)(2,1)S(1)} %collective-permute-done.5.refs_0_, bf16[512,256]{1,0:T(8,128)(2,1)S(1)} %collective-permute-done.6.refs_1_, bf16[512,256]{1,0:T(8,128)(2,1)S(1)} %collective-permute-done.11.refs_2_, ...), custom_call_target="tpu_custom_call", output_to_operand_aliasing={{0}: (6, {}), {1}: (7, {})} | custom-call | flops 1 | bytes 1 | tf_op jit(solution)/shard_map/pallas_call | solution.py:49
  35.0 2.2 %shard_map.109 = (f32[512,1024]{1,0:T(8,128)S(1)}, f32[512,1024]{1,0:T(8,128)S(1)}) custom-call(bf16[256,256]{1,0:T(8,128)(2,1)S(1)} %collective-permute-done.9.refs_0_, bf16[256,256]{1,0:T(8,128)(2,1)S(1)} %collective-permute-done.10.refs_1_, bf16[512,256]{1,0:T(8,128)(2,1)S(1)} %collective-permute-done.15.refs_2_, ...), custom_call_target="tpu_custom_call", output_to_operand_aliasing={{0}: (6, {}), {1}: (7, {})} | custom-call | flops 1 | bytes 1 | tf_op jit(solution)/shard_map/pallas_call | solution.py:49
  37.2 1.9 %shard_map.110 = (f32[512,1024]{1,0:T(8,128)S(1)}, f32[512,1024]{1,0:T(8,128)S(1)}, bf16[512,1024]{1,0:T(8,128)(2,1)S(1)}) custom-call(bf16[256,256]{1,0:T(8,128)(2,1)S(1)} %collective-permute-done.13.refs_0_, bf16[256,256]{1,0:T(8,128)(2,1)S(1)} %collective-permute-done.14.refs_1_, ...), custom_call_target="tpu_custom_call", output_to_operand_aliasing={{0}: (4, {}), {1}: (5, {})} | custom-call | flops 1 | bytes 1 | tf_op jit(solution)/shard_map/pallas_call | solution.py:49
  45.5 1.8 %collective-permute-done.18 = bf16[256,256]{1,0:T(8,128)(2,1)S(1)} collective-permute-done((bf16[256,256]{1,0:T(8,128)(2,1)S(1)}, bf16[256,256]{1,0:T(8,128)(2,1)S(1)}, u32[]{:S(2)}, u32[]{:S(2)}) %collective-permute-start.18) | collective-permute-done | bytes 131104 | tf_op jit(solution)/shard_map/ppermute | solution.py:299
  51.8 3.7 %collective-permute-done.21 = bf16[512,256]{1,0:T(8,128)(2,1)S(1)} collective-permute-done((bf16[512,256]{1,0:T(8,128)(2,1)S(1)}, bf16[512,256]{1,0:T(8,128)(2,1)S(1)}, u32[]{:S(2)}, u32[]{:S(2)}) %collective-permute-start.21) | collective-permute-done | bytes 262176 | tf_op jit(solution)/shard_map/ppermute | solution.py:299
  56.9 1.7 %collective-permute-start.24 = (bf16[512,256]{1,0:T(8,128)(2,1)S(1)}, bf16[512,256]{1,0:T(8,128)(2,1)S(1)}, u32[]{:S(2)}, u32[]{:S(2)}) collective-permute-start(bf16[512,256]{1,0:T(8,128)(2,1)S(1)} %add_convert_fusion.9), channel_id=1, source_target_pairs={{0,4},{1,5},{4,8},{5,9},{8,12},{9,13},{12,14},{13,15},{14,10},{15,... | collective-permute-start | bytes 786440 | tf_op jit(solution)/shard_map/ppermute | solution.py:299
  60.6 2.8 %collective-permute-done.24 = bf16[512,256]{1,0:T(8,128)(2,1)S(1)} collective-permute-done((bf16[512,256]{1,0:T(8,128)(2,1)S(1)}, bf16[512,256]{1,0:T(8,128)(2,1)S(1)}, u32[]{:S(2)}, u32[]{:S(2)}) %collective-permute-start.24) | collective-permute-done | bytes 262176 | tf_op jit(solution)/shard_map/ppermute | solution.py:299
  63.3 2.0 %collective-permute-done.31 = bf16[512,256]{1,0:T(8,128)(2,1)S(1)} collective-permute-done((bf16[512,256]{1,0:T(8,128)(2,1)S(1)}, bf16[512,256]{1,0:T(8,128)(2,1)S(1)}, u32[]{:S(2)}, u32[]{:S(2)}) %collective-permute-start.31) | collective-permute-done | bytes 262176 | tf_op jit(solution)/shard_map/ppermute | solution.py:300
  68.1 3.9 %collective-permute-done.32.refs_3_ = bf16[512,256]{1,0:T(8,128)(2,1)S(1)} collective-permute-done((bf16[512,256]{1,0:T(8,128)(2,1)S(1)}, bf16[512,256]{1,0:T(8,128)(2,1)S(1)}, u32[]{:S(2)}, u32[]{:S(2)}) %collective-permute-start.32) | collective-permute-done | bytes 262176 | tf_op jit(solution)/shard_map/ppermute | solution.py:300
  75.0 1.8 %shard_map.119 = (f32[512,1024]{1,0:T(8,128)S(1)}, f32[512,1024]{1,0:T(8,128)S(1)}, f32[512,1024]{1,0:T(8,128)S(1)}) custom-call(f32[512,1024]{1,0:T(8,128)S(1)} %get-tuple-element.203.refs_0_, f32[512,1024]{1,0:T(8,128)S(1)} %get-tuple-element.204.refs_1_, s32[1,1024]{1,0:T(1,128)S(1)} %copy-done.2, s32[1,1024]{1,0:T(1,128)S(1)} %copy-done.3), custom_call_target="tpu_custom_call" | custom-call | flops 268435456 | bytes 524288 | tf_op jit(solution)/shard_map/pallas_call | solution.py:49
  76.8 2.5 %collective-permute-done.36.refs_1_ = bf16[512,256]{1,0:T(8,128)(2,1)S(1)} collective-permute-done((bf16[512,256]{1,0:T(8,128)(2,1)S(1)}, bf16[512,256]{1,0:T(8,128)(2,1)S(1)}, u32[]{:S(2)}, u32[]{:S(2)}) %collective-permute-start.36) | collective-permute-done | bytes 262176 | tf_op jit(solution)/shard_map/ppermute | solution.py:300
  83.2 2.5 %collective-permute-done.37.refs_1_ = bf16[512,256]{1,0:T(8,128)(2,1)S(1)} collective-permute-done((bf16[512,256]{1,0:T(8,128)(2,1)S(1)}, bf16[512,256]{1,0:T(8,128)(2,1)S(1)}, u32[]{:S(2)}, u32[]{:S(2)}) %collective-permute-start.37) | collective-permute-done | bytes 262176 | tf_op jit(solution)/shard_map/ppermute | solution.py:300
  89.7 2.3 %collective-permute-done.40.refs_1_ = bf16[512,256]{1,0:T(8,128)(2,1)S(1)} collective-permute-done((bf16[512,256]{1,0:T(8,128)(2,1)S(1)}, bf16[512,256]{1,0:T(8,128)(2,1)S(1)}, u32[]{:S(2)}, u32[]{:S(2)}) %collective-permute-start.40) | collective-permute-done | bytes 262176 | tf_op jit(solution)/shard_map/ppermute | solution.py:300
  103.9 1.8 %shard_map.126 = (f32[512,256]{1,0:T(8,128)S(1)}, bf16[512,256]{1,0:T(8,128)(2,1)S(1)}, bf16[512,256]{1,0:T(8,128)(2,1)S(1)}) custom-call(bf16[512,1024]{1,0:T(8,128)(2,1)S(1)} %get-tuple-element.252.refs_0_, bf16[512,1024]{1,0:T(8,128)(2,1)S(1)} %get-tuple-element.219.refs_1_, bf16[4096,1024]{1,0:T(8,128)(2,1)S(1)} %get-tuple-element.134.refs_4_.refs_2_, ...), custom_call_target="tpu_custom_call" | custom-call | flops 1610612736 | bytes 3145728 | tf_op jit(solution)/shard_map/pallas_call | solution.py:49
  108.5 2.4 %shard_map.129 = (f32[512,256]{1,0:T(8,128)S(1)}, f32[512,256]{1,0:T(8,128)S(1)}, bf16[512,256]{1,0:T(8,128)(2,1)S(1)}, bf16[512,256]{1,0:T(8,128)(2,1)S(1)}) custom-call(bf16[512,1024]{1,0:T(8,128)(2,1)S(1)} %get-tuple-element.252.refs_0_, bf16[512,1024]{1,0:T(8,128)(2,1)S(1)} %get-tuple-element.219.refs_1_, ...), custom_call_target="tpu_custom_call" | custom-call | flops 2147483648 | bytes 4194304 | tf_op jit(solution)/shard_map/pallas_call | solution.py:49
  115.2 2.4 %shard_map.130 = (f32[512,256]{1,0:T(8,128)S(1)}, f32[512,256]{1,0:T(8,128)S(1)}, bf16[512,256]{1,0:T(8,128)(2,1)S(1)}, bf16[512,256]{1,0:T(8,128)(2,1)S(1)}) custom-call(bf16[512,1024]{1,0:T(8,128)(2,1)S(1)} %get-tuple-element.252.refs_0_, bf16[512,1024]{1,0:T(8,128)(2,1)S(1)} %get-tuple-element.219.refs_1_, ...), custom_call_target="tpu_custom_call" | custom-call | flops 2147483648 | bytes 4194304 | tf_op jit(solution)/shard_map/pallas_call | solution.py:49
  117.6 2.8 %collective-permute-done.55 = bf16[512,256]{1,0:T(8,128)(2,1)S(1)} collective-permute-done((bf16[512,256]{1,0:T(8,128)(2,1)S(1)}, bf16[512,256]{1,0:T(8,128)(2,1)S(1)}, u32[]{:S(2)}, u32[]{:S(2)}) %collective-permute-start.55) | collective-permute-done | bytes 262176 | tf_op jit(solution)/shard_map/ppermute | solution.py:299
  125.2 2.4 %collective-permute-done.58 = bf16[512,256]{1,0:T(8,128)(2,1)S(1)} collective-permute-done((bf16[512,256]{1,0:T(8,128)(2,1)S(1)}, bf16[512,256]{1,0:T(8,128)(2,1)S(1)}, u32[]{:S(2)}, u32[]{:S(2)}) %collective-permute-start.58) | collective-permute-done | bytes 262176 | tf_op jit(solution)/shard_map/ppermute | solution.py:299
  127.6 2.1 %collective-permute-done.65 = bf16[512,256]{1,0:T(8,128)(2,1)S(1)} collective-permute-done((bf16[512,256]{1,0:T(8,128)(2,1)S(1)}, bf16[512,256]{1,0:T(8,128)(2,1)S(1)}, u32[]{:S(2)}, u32[]{:S(2)}) %collective-permute-start.65) | collective-permute-done | bytes 262176 | tf_op jit(solution)/shard_map/ppermute | solution.py:300
  130.1 1.9 %collective-permute-start.63 = (bf16[512,256]{1,0:T(8,128)(2,1)S(1)}, bf16[512,256]{1,0:T(8,128)(2,1)S(1)}, u32[]{:S(2)}, u32[]{:S(2)}) collective-permute-start(bf16[512,256]{1,0:T(8,128)(2,1)S(1)} %add_convert_fusion.2), channel_id=1, source_target_pairs={{0,4},{1,5},{4,8},{5,9},{8,12},{9,13},{12,14},{13,15},{14,10},{15,... | collective-permute-start | bytes 786440 | tf_op jit(solution)/shard_map/ppermute | solution.py:299
  132.0 3.4 %collective-permute-start.33 = (bf16[512,256]{1,0:T(8,128)(2,1)S(1)}, bf16[512,256]{1,0:T(8,128)(2,1)S(1)}, u32[]{:S(2)}, u32[]{:S(2)}) collective-permute-start(bf16[512,256]{1,0:T(8,128)(2,1)S(1)} %get-tuple-element.200), channel_id=1, source_target_pairs={{0,16},{1,17},{2,18},{3,19},{4,20},{5,21},{6,22},{7,23},{8,24},{9,... | collective-permute-start | bytes 786440 | tf_op jit(solution)/shard_map/ppermute | solution.py:426
  138.0 3.7 %collective-permute-done.33 = bf16[512,256]{1,0:T(8,128)(2,1)S(1)} collective-permute-done((bf16[512,256]{1,0:T(8,128)(2,1)S(1)}, bf16[512,256]{1,0:T(8,128)(2,1)S(1)}, u32[]{:S(2)}, u32[]{:S(2)}) %collective-permute-start.33) | collective-permute-done | bytes 262176 | tf_op jit(solution)/shard_map/ppermute | solution.py:426
  142.5 3.5 %collective-permute-done.67 = bf16[512,256]{1,0:T(8,128)(2,1)S(1)} collective-permute-done((bf16[512,256]{1,0:T(8,128)(2,1)S(1)}, bf16[512,256]{1,0:T(8,128)(2,1)S(1)}, u32[]{:S(2)}, u32[]{:S(2)}) %collective-permute-start.67) | collective-permute-done | bytes 262176 | tf_op jit(solution)/shard_map/ppermute | solution.py:463
  (178 shorter events, 62.6 us)
Async XLA Ops:
  2.0 9.4 %collective-permute-start.1 = (bf16[512,256]{1,0:T(8,128)(2,1)S(1)}, bf16[512,256]{1,0:T(8,128)(2,1)S(1)}, u32[]{:S(2)}, u32[]{:S(2)}) collective-permute-start(bf16[512,256]{1,0:T(8,128)(2,1)S(1)} %shard_map.104.refs_2_.refs_4_), channel_id=1, source_target_pairs={{4,0},{5,1},{8,4},{9,5},{12,8},{13,9},{14,12},{15,13},{10,14},{11,... | collective-permute-start | bytes 786440 | tf_op jit(solution)/shard_map/ppermute | solution.py:300
  5.0 8.0 %collective-permute-start = (bf16[512,256]{1,0:T(8,128)(2,1)S(1)}, bf16[512,256]{1,0:T(8,128)(2,1)S(1)}, u32[]{:S(2)}, u32[]{:S(2)}) collective-permute-start(bf16[512,256]{1,0:T(8,128)(2,1)S(1)} %shard_map.104.refs_2_.refs_4_), channel_id=1, source_target_pairs={{0,4},{1,5},{4,8},{5,9},{8,12},{9,13},{12,14},{13,15},{14,10},{15,... | collective-permute-start | bytes 786440 | tf_op jit(solution)/shard_map/ppermute | solution.py:299
  5.2 8.8 %collective-permute-start.4 = (bf16[512,256]{1,0:T(8,128)(2,1)S(1)}, bf16[512,256]{1,0:T(8,128)(2,1)S(1)}, u32[]{:S(2)}, u32[]{:S(2)}) collective-permute-start(bf16[512,256]{1,0:T(8,128)(2,1)S(1)} %shard_map.104.refs_2_.refs_4_), channel_id=1, source_target_pairs={{0,1},{1,0},{4,5},{5,4},{8,9},{9,8},{12,13},{13,12},{14,15},{15,14... | collective-permute-start | bytes 786440 | tf_op jit(solution)/shard_map/ppermute | solution.py:301
  11.4 8.6 %collective-permute-start.3 = (bf16[512,256]{1,0:T(8,128)(2,1)S(1)}, bf16[512,256]{1,0:T(8,128)(2,1)S(1)}, u32[]{:S(2)}, u32[]{:S(2)}) collective-permute-start(bf16[512,256]{1,0:T(8,128)(2,1)S(1)} %collective-permute-done.1.refs_1_), channel_id=1, source_target_pairs={{4,0},{5,1},{8,4},{9,5},{12,8},{13,9},{14,12},{15,13},{10,14},{11,... | collective-permute-start | bytes 786440 | tf_op jit(solution)/shard_map/ppermute | solution.py:300
  13.1 8.6 %collective-permute-start.2 = (bf16[512,256]{1,0:T(8,128)(2,1)S(1)}, bf16[512,256]{1,0:T(8,128)(2,1)S(1)}, u32[]{:S(2)}, u32[]{:S(2)}) collective-permute-start(bf16[512,256]{1,0:T(8,128)(2,1)S(1)} %collective-permute-done.refs_0_), channel_id=1, source_target_pairs={{0,4},{1,5},{4,8},{5,9},{8,12},{9,13},{12,14},{13,15},{14,10},{15,... | collective-permute-start | bytes 786440 | tf_op jit(solution)/shard_map/ppermute | solution.py:299
  13.4 8.6 %collective-permute-start.7 = (bf16[512,256]{1,0:T(8,128)(2,1)S(1)}, bf16[512,256]{1,0:T(8,128)(2,1)S(1)}, u32[]{:S(2)}, u32[]{:S(2)}) collective-permute-start(bf16[512,256]{1,0:T(8,128)(2,1)S(1)} %collective-permute-done.refs_0_), channel_id=1, source_target_pairs={{0,1},{1,0},{4,5},{5,4},{8,9},{9,8},{12,13},{13,12},{14,15},{15,14... | collective-permute-start | bytes 786440 | tf_op jit(solution)/shard_map/ppermute | solution.py:301
  13.4 9.1 %collective-permute-start.8 = (bf16[512,256]{1,0:T(8,128)(2,1)S(1)}, bf16[512,256]{1,0:T(8,128)(2,1)S(1)}, u32[]{:S(2)}, u32[]{:S(2)}) collective-permute-start(bf16[512,256]{1,0:T(8,128)(2,1)S(1)} %collective-permute-done.1.refs_1_), channel_id=1, source_target_pairs={{0,1},{1,0},{4,5},{5,4},{8,9},{9,8},{12,13},{13,12},{14,15},{15,14... | collective-permute-start | bytes 786440 | tf_op jit(solution)/shard_map/ppermute | solution.py:301
  20.0 7.8 %collective-permute-start.6 = (bf16[512,256]{1,0:T(8,128)(2,1)S(1)}, bf16[512,256]{1,0:T(8,128)(2,1)S(1)}, u32[]{:S(2)}, u32[]{:S(2)}) collective-permute-start(bf16[512,256]{1,0:T(8,128)(2,1)S(1)} %collective-permute-done.3.refs_1_), channel_id=1, source_target_pairs={{4,0},{5,1},{8,4},{9,5},{12,8},{13,9},{14,12},{15,13},{10,14},{11,... | collective-permute-start | bytes 786440 | tf_op jit(solution)/shard_map/ppermute | solution.py:300
  21.6 7.8 %collective-permute-start.5 = (bf16[512,256]{1,0:T(8,128)(2,1)S(1)}, bf16[512,256]{1,0:T(8,128)(2,1)S(1)}, u32[]{:S(2)}, u32[]{:S(2)}) collective-permute-start(bf16[512,256]{1,0:T(8,128)(2,1)S(1)} %collective-permute-done.2.refs_0_), channel_id=1, source_target_pairs={{0,4},{1,5},{4,8},{5,9},{8,12},{9,13},{12,14},{13,15},{14,10},{15,... | collective-permute-start | bytes 786440 | tf_op jit(solution)/shard_map/ppermute | solution.py:299
  22.0 7.9 %collective-permute-start.11 = (bf16[512,256]{1,0:T(8,128)(2,1)S(1)}, bf16[512,256]{1,0:T(8,128)(2,1)S(1)}, u32[]{:S(2)}, u32[]{:S(2)}) collective-permute-start(bf16[512,256]{1,0:T(8,128)(2,1)S(1)} %collective-permute-done.2.refs_0_), channel_id=1, source_target_pairs={{0,1},{1,0},{4,5},{5,4},{8,9},{9,8},{12,13},{13,12},{14,15},{15,14... | collective-permute-start | bytes 786440 | tf_op jit(solution)/shard_map/ppermute | solution.py:301
  22.0 8.4 %collective-permute-start.12 = (bf16[512,256]{1,0:T(8,128)(2,1)S(1)}, bf16[512,256]{1,0:T(8,128)(2,1)S(1)}, u32[]{:S(2)}, u32[]{:S(2)}) collective-permute-start(bf16[512,256]{1,0:T(8,128)(2,1)S(1)} %collective-permute-done.3.refs_1_), channel_id=1, source_target_pairs={{0,1},{1,0},{4,5},{5,4},{8,9},{9,8},{12,13},{13,12},{14,15},{15,14... | collective-permute-start | bytes 786440 | tf_op jit(solution)/shard_map/ppermute | solution.py:301
  40.8 6.8 %collective-permute-start.20 = (bf16[512,256]{1,0:T(8,128)(2,1)S(1)}, bf16[512,256]{1,0:T(8,128)(2,1)S(1)}, u32[]{:S(2)}, u32[]{:S(2)}) collective-permute-start(bf16[512,256]{1,0:T(8,128)(2,1)S(1)} %get-tuple-element.172), channel_id=1, source_target_pairs={{0,1},{1,0},{4,5},{5,4},{8,9},{9,8},{12,13},{13,12},{14,15},{15,14... | collective-permute-start | bytes 786440 | tf_op jit(solution)/shard_map/ppermute | solution.py:301
  47.8 7.7 %collective-permute-start.21 = (bf16[512,256]{1,0:T(8,128)(2,1)S(1)}, bf16[512,256]{1,0:T(8,128)(2,1)S(1)}, u32[]{:S(2)}, u32[]{:S(2)}) collective-permute-start(bf16[512,256]{1,0:T(8,128)(2,1)S(1)} %pad_maximum_fusion), channel_id=1, source_target_pairs={{0,4},{1,5},{4,8},{5,9},{8,12},{9,13},{12,14},{13,15},{14,10},{15,... | collective-permute-start | bytes 786440 | tf_op jit(solution)/shard_map/ppermute | solution.py:299
  49.5 7.3 %collective-permute-start.26 = (bf16[512,256]{1,0:T(8,128)(2,1)S(1)}, bf16[512,256]{1,0:T(8,128)(2,1)S(1)}, u32[]{:S(2)}, u32[]{:S(2)}) collective-permute-start(bf16[512,256]{1,0:T(8,128)(2,1)S(1)} %pad_maximum_fusion.1), channel_id=1, source_target_pairs={{4,0},{5,1},{8,4},{9,5},{12,8},{13,9},{14,12},{15,13},{10,14},{11,... | collective-permute-start | bytes 786440 | tf_op jit(solution)/shard_map/ppermute | solution.py:300
  50.0 6.8 %collective-permute-start.19 = (bf16[512,256]{1,0:T(8,128)(2,1)S(1)}, bf16[512,256]{1,0:T(8,128)(2,1)S(1)}, u32[]{:S(2)}, u32[]{:S(2)}) collective-permute-start(bf16[512,256]{1,0:T(8,128)(2,1)S(1)} %get-tuple-element.170), channel_id=1, source_target_pairs={{0,1},{1,0},{4,5},{5,4},{8,9},{9,8},{12,13},{13,12},{14,15},{15,14... | collective-permute-start | bytes 786440 | tf_op jit(solution)/shard_map/ppermute | solution.py:301
  50.0 8.5 %collective-permute-start.25 = (bf16[512,256]{1,0:T(8,128)(2,1)S(1)}, bf16[512,256]{1,0:T(8,128)(2,1)S(1)}, u32[]{:S(2)}, u32[]{:S(2)}) collective-permute-start(bf16[512,256]{1,0:T(8,128)(2,1)S(1)} %get-tuple-element.177), channel_id=1, source_target_pairs={{0,1},{1,0},{4,5},{5,4},{8,9},{9,8},{12,13},{13,12},{14,15},{15,14... | collective-permute-start | bytes 786440 | tf_op jit(solution)/shard_map/ppermute | solution.py:301
  58.7 6.7 %collective-permute-start.31 = (bf16[512,256]{1,0:T(8,128)(2,1)S(1)}, bf16[512,256]{1,0:T(8,128)(2,1)S(1)}, u32[]{:S(2)}, u32[]{:S(2)}) collective-permute-start(bf16[512,256]{1,0:T(8,128)(2,1)S(1)} %add_convert_fusion.8), channel_id=1, source_target_pairs={{4,0},{5,1},{8,4},{9,5},{12,8},{13,9},{14,12},{15,13},{10,14},{11,... | collective-permute-start | bytes 786440 | tf_op jit(solution)/shard_map/ppermute | solution.py:300
  65.6 6.4 %collective-permute-start.32 = (bf16[512,256]{1,0:T(8,128)(2,1)S(1)}, bf16[512,256]{1,0:T(8,128)(2,1)S(1)}, u32[]{:S(2)}, u32[]{:S(2)}) collective-permute-start(bf16[512,256]{1,0:T(8,128)(2,1)S(1)} %add_convert_fusion.6), channel_id=1, source_target_pairs={{4,0},{5,1},{8,4},{9,5},{12,8},{13,9},{14,12},{15,13},{10,14},{11,... | collective-permute-start | bytes 786440 | tf_op jit(solution)/shard_map/ppermute | solution.py:300
  75.0 6.9 %collective-permute-start.38 = (bf16[512,256]{1,0:T(8,128)(2,1)S(1)}, bf16[512,256]{1,0:T(8,128)(2,1)S(1)}, u32[]{:S(2)}, u32[]{:S(2)}) collective-permute-start(bf16[512,256]{1,0:T(8,128)(2,1)S(1)} %get-tuple-element.201.refs_2_), channel_id=1, source_target_pairs={{0,1},{1,0},{4,5},{5,4},{8,9},{9,8},{12,13},{13,12},{14,15},{15,14... | collective-permute-start | bytes 786440 | tf_op jit(solution)/shard_map/ppermute | solution.py:301
  79.8 6.5 %collective-permute-start.35 = (bf16[512,256]{1,0:T(8,128)(2,1)S(1)}, bf16[512,256]{1,0:T(8,128)(2,1)S(1)}, u32[]{:S(2)}, u32[]{:S(2)}) collective-permute-start(bf16[512,256]{1,0:T(8,128)(2,1)S(1)} %collective-permute-done.34.refs_0_), channel_id=1, source_target_pairs={{0,4},{1,5},{4,8},{5,9},{8,12},{9,13},{12,14},{13,15},{14,10},{15,... | collective-permute-start | bytes 786440 | tf_op jit(solution)/shard_map/ppermute | solution.py:299
  81.3 6.5 %collective-permute-start.42 = (bf16[512,256]{1,0:T(8,128)(2,1)S(1)}, bf16[512,256]{1,0:T(8,128)(2,1)S(1)}, u32[]{:S(2)}, u32[]{:S(2)}) collective-permute-start(bf16[512,256]{1,0:T(8,128)(2,1)S(1)} %collective-permute-done.36.refs_1_), channel_id=1, source_target_pairs={{0,1},{1,0},{4,5},{5,4},{8,9},{9,8},{12,13},{13,12},{14,15},{15,14... | collective-permute-start | bytes 786440 | tf_op jit(solution)/shard_map/ppermute | solution.py:301
  81.4 7.0 %collective-permute-start.41 = (bf16[512,256]{1,0:T(8,128)(2,1)S(1)}, bf16[512,256]{1,0:T(8,128)(2,1)S(1)}, u32[]{:S(2)}, u32[]{:S(2)}) collective-permute-start(bf16[512,256]{1,0:T(8,128)(2,1)S(1)} %collective-permute-done.34.refs_0_), channel_id=1, source_target_pairs={{0,1},{1,0},{4,5},{5,4},{8,9},{9,8},{12,13},{13,12},{14,15},{15,14... | collective-permute-start | bytes 786440 | tf_op jit(solution)/shard_map/ppermute | solution.py:301
  87.8 7.0 %collective-permute-start.47 = (bf16[512,256]{1,0:T(8,128)(2,1)S(1)}, bf16[512,256]{1,0:T(8,128)(2,1)S(1)}, u32[]{:S(2)}, u32[]{:S(2)}) collective-permute-start(bf16[512,256]{1,0:T(8,128)(2,1)S(1)} %collective-permute-done.35.refs_0_), channel_id=1, source_target_pairs={{0,1},{1,0},{4,5},{5,4},{8,9},{9,8},{12,13},{13,12},{14,15},{15,14... | collective-permute-start | bytes 786440 | tf_op jit(solution)/shard_map/ppermute | solution.py:301
  87.8 7.4 %collective-permute-start.48 = (bf16[512,256]{1,0:T(8,128)(2,1)S(1)}, bf16[512,256]{1,0:T(8,128)(2,1)S(1)}, u32[]{:S(2)}, u32[]{:S(2)}) collective-permute-start(bf16[512,256]{1,0:T(8,128)(2,1)S(1)} %collective-permute-done.37.refs_1_), channel_id=1, source_target_pairs={{0,1},{1,0},{4,5},{5,4},{8,9},{9,8},{12,13},{13,12},{14,15},{15,14... | collective-permute-start | bytes 786440 | tf_op jit(solution)/shard_map/ppermute | solution.py:301
  105.8 6.5 %collective-permute-start.54 = (bf16[512,256]{1,0:T(8,128)(2,1)S(1)}, bf16[512,256]{1,0:T(8,128)(2,1)S(1)}, u32[]{:S(2)}, u32[]{:S(2)}) collective-permute-start(bf16[512,256]{1,0:T(8,128)(2,1)S(1)} %get-tuple-element.232), channel_id=1, source_target_pairs={{0,1},{1,0},{4,5},{5,4},{8,9},{9,8},{12,13},{13,12},{14,15},{15,14... | collective-permute-start | bytes 786440 | tf_op jit(solution)/shard_map/ppermute | solution.py:301
  106.0 7.9 %collective-permute-start.56 = (bf16[512,256]{1,0:T(8,128)(2,1)S(1)}, bf16[512,256]{1,0:T(8,128)(2,1)S(1)}, u32[]{:S(2)}, u32[]{:S(2)}) collective-permute-start(bf16[512,256]{1,0:T(8,128)(2,1)S(1)} %get-tuple-element.235), channel_id=1, source_target_pairs={{0,1},{1,0},{4,5},{5,4},{8,9},{9,8},{12,13},{13,12},{14,15},{15,14... | collective-permute-start | bytes 786440 | tf_op jit(solution)/shard_map/ppermute | solution.py:301
  112.4 8.0 %collective-permute-start.55 = (bf16[512,256]{1,0:T(8,128)(2,1)S(1)}, bf16[512,256]{1,0:T(8,128)(2,1)S(1)}, u32[]{:S(2)}, u32[]{:S(2)}) collective-permute-start(bf16[512,256]{1,0:T(8,128)(2,1)S(1)} %pad_maximum_fusion.2), channel_id=1, source_target_pairs={{0,4},{1,5},{4,8},{5,9},{8,12},{9,13},{12,14},{13,15},{14,10},{15,... | collective-permute-start | bytes 786440 | tf_op jit(solution)/shard_map/ppermute | solution.py:299
  114.1 7.0 %collective-permute-start.60 = (bf16[512,256]{1,0:T(8,128)(2,1)S(1)}, bf16[512,256]{1,0:T(8,128)(2,1)S(1)}, u32[]{:S(2)}, u32[]{:S(2)}) collective-permute-start(bf16[512,256]{1,0:T(8,128)(2,1)S(1)} %pad_maximum_fusion.3), channel_id=1, source_target_pairs={{4,0},{5,1},{8,4},{9,5},{12,8},{13,9},{14,12},{15,13},{10,14},{11,... | collective-permute-start | bytes 786440 | tf_op jit(solution)/shard_map/ppermute | solution.py:300
  114.7 8.1 %collective-permute-start.59 = (bf16[512,256]{1,0:T(8,128)(2,1)S(1)}, bf16[512,256]{1,0:T(8,128)(2,1)S(1)}, u32[]{:S(2)}, u32[]{:S(2)}) collective-permute-start(bf16[512,256]{1,0:T(8,128)(2,1)S(1)} %get-tuple-element.237), channel_id=1, source_target_pairs={{0,1},{1,0},{4,5},{5,4},{8,9},{9,8},{12,13},{13,12},{14,15},{15,14... | collective-permute-start | bytes 786440 | tf_op jit(solution)/shard_map/ppermute | solution.py:301
  123.0 6.8 %collective-permute-start.65 = (bf16[512,256]{1,0:T(8,128)(2,1)S(1)}, bf16[512,256]{1,0:T(8,128)(2,1)S(1)}, u32[]{:S(2)}, u32[]{:S(2)}) collective-permute-start(bf16[512,256]{1,0:T(8,128)(2,1)S(1)} %add_convert_fusion.3), channel_id=1, source_target_pairs={{4,0},{5,1},{8,4},{9,5},{12,8},{13,9},{14,12},{15,13},{10,14},{11,... | collective-permute-start | bytes 786440 | tf_op jit(solution)/shard_map/ppermute | solution.py:300
  132.0 9.6 %collective-permute-start.33 = (bf16[512,256]{1,0:T(8,128)(2,1)S(1)}, bf16[512,256]{1,0:T(8,128)(2,1)S(1)}, u32[]{:S(2)}, u32[]{:S(2)}) collective-permute-start(bf16[512,256]{1,0:T(8,128)(2,1)S(1)} %get-tuple-element.200), channel_id=1, source_target_pairs={{0,16},{1,17},{2,18},{3,19},{4,20},{5,21},{6,22},{7,23},{8,24},{9,... | collective-permute-start | bytes 786440 | tf_op jit(solution)/shard_map/ppermute | solution.py:426
  136.7 9.3 %collective-permute-start.67 = (bf16[512,256]{1,0:T(8,128)(2,1)S(1)}, bf16[512,256]{1,0:T(8,128)(2,1)S(1)}, u32[]{:S(2)}, u32[]{:S(2)}) collective-permute-start(bf16[512,256]{1,0:T(8,128)(2,1)S(1)} %add_convert_fusion), channel_id=1, source_target_pairs={{16,0},{17,1},{18,2},{19,3},{20,4},{21,5},{22,6},{23,7},{24,8},{25... | collective-permute-start | bytes 786440 | tf_op jit(solution)/shard_map/ppermute | solution.py:463
  (42 other events, 225.6 us)
